TPU v7x, 512 devices: a whole 4x8x8 slice. The times are simulated.
512 devices in a mesh: dp: 16 (over x, y_hi), ep: 32 (over y_lo, z, core).
Axes of the slice: x: 4, y: 8 (y_hi: 4, y_lo: 2; y = y_hi * 2 + y_lo), z: 8, core: 2. Of those that a mesh axis runs over, the one named last changes fastest.
Arguments:
- expert_inputs: bfloat16 [163840, 3584], P(('dp', 'ep')), may hold values from -6 to 6
- hidden_grads: bfloat16 [163840, 256], P(('dp', 'ep')), may hold values from -3 to 3
- row_counts: int32 [16384], P(('dp', 'ep')), may hold values from 0 to 10, as said below
- top_ids: int32 [65536, 8], P(('dp', 'ep')), may hold values from 0 to 383, as said below
- route_slots: int32 [65536, 8], P(('dp', 'ep')), may hold values from -1 to 9, as said below
- master_weights: float32 [32, 3584, 256], P('ep', 'dp'), may hold values from -0.125 to 0.125
- first_moment: float32 [32, 3584, 256], P('ep', 'dp'), may hold values from -6 to 6
- second_moment: float32 [32, 3584, 256], P('ep', 'dp'), may hold values from 0.05 to 2
Outputs:
- input_grads: bfloat16 [65536, 3584], P(('dp', 'ep'))
- new_master: float32 [32, 3584, 256], P('ep', 'dp')
- new_first: float32 [32, 3584, 256], P('ep', 'dp')
- new_second: float32 [32, 3584, 256], P('ep', 'dp')
Inputs may be any that keep to these rules, and one draw needn't show every extreme that they name: `row_counts`: row counts of each (replica, expert, source device) block; equal on the 8 devices of one expert, equal to the number of that source's routes to that expert with route_slots >= 0, and 10 is reached in every draw. `top_ids`: each token names 8 different experts; only ids below 4 lie in the window. `route_slots`: -1 for routes outside the window or over capacity; a source device's kept routes to one expert take rows 0 to count - 1 in token order.
All inputs are finite; a program needn't handle non-finite values.
Results may differ from a plain program's by a relative error of at most 0.02.
Values may be sent and summed in bfloat16 or wider, within the bound.
A program may use at most 64 MiB of HBM per device.

v0:
```python
import jax
import jax.numpy as jnp
from jax import lax
from jax.sharding import PartitionSpec as P

HIDDEN_SIZE = 2048


beta_one = 0.9
beta_two = 0.999
learn_rate = 0.001
adam_epsilon = 1e-08
weight_decay = 0.1
step_count = 100


def update_weights(expert_inputs, masked_grads, master_weights, first_moment, second_moment):
    grad_rows = lax.psum_scatter(
        lax.dot_general(
            expert_inputs,
            masked_grads,
            (((0,), (0,)), ((), ())),
            preferred_element_type=jnp.float32,
        ).astype(jnp.bfloat16),
        "dp",
        scatter_dimension=0,
        tiled=True,
    ).astype(jnp.float32)
    master_here = master_weights[0]
    new_first = beta_one * first_moment[0] + (1.0 - beta_one) * grad_rows
    new_second = beta_two * second_moment[0] + (1.0 - beta_two) * grad_rows * grad_rows
    first_hat = new_first / (1.0 - beta_one**step_count)
    second_hat = new_second / (1.0 - beta_two**step_count)
    new_master = master_here - learn_rate * (
        first_hat / (jnp.sqrt(second_hat) + adam_epsilon) + weight_decay * master_here
    )
    return (new_master[None], new_first[None], new_second[None])


def return_rows(hidden_grads, current_bf, top_ids, route_slots, capacity, slice_count):
    partial_rows = lax.dot_general(
        hidden_grads,
        lax.all_gather(current_bf, "dp", axis=0, tiled=True),
        (((1,), (1,)), ((), ())),
        preferred_element_type=jnp.float32,
    ).astype(jnp.bfloat16)
    received = lax.all_to_all(partial_rows, "ep", split_axis=0, concat_axis=0, tiled=True)
    token_count = top_ids.shape[0]
    columns = lax.broadcasted_iota(jnp.int32, (token_count, received.shape[0]), 1)
    column_expert = columns // (capacity * slice_count)
    column_slot = columns % capacity
    matches = jnp.zeros((token_count, received.shape[0]), jnp.bool_)
    for route in range(top_ids.shape[1]):
        expert_id = top_ids[:, route : route + 1]
        slot_id = route_slots[:, route : route + 1]
        matches = matches | (column_expert == expert_id) & (column_slot == slot_id) & (slot_id >= 0)
    combine_table = matches.astype(jnp.bfloat16)
    return jnp.dot(combine_table, received, preferred_element_type=jnp.float32).astype(jnp.bfloat16)


def body(
    expert_inputs,
    hidden_grads,
    row_counts,
    top_ids,
    route_slots,
    master_weights,
    first_moment,
    second_moment,
):
    groups = lax.axis_size("ep")
    capacity = expert_inputs.shape[0] // groups
    slice_count = HIDDEN_SIZE // hidden_grads.shape[1]
    current_bf = master_weights[0].astype(jnp.bfloat16)
    live_rows = lax.broadcasted_iota(jnp.int32, (groups, capacity), 1) < row_counts[:, None]
    live_rows = live_rows.reshape(groups * capacity, 1)
    masked_grads = jnp.where(live_rows, hidden_grads, jnp.zeros_like(hidden_grads))
    input_grads = return_rows(hidden_grads, current_bf, top_ids, route_slots, capacity, slice_count)
    new_master, new_first, new_second = update_weights(
        expert_inputs, masked_grads, master_weights, first_moment, second_moment
    )
    return (input_grads, new_master, new_first, new_second)


def solution(mesh):
    in_specs = (
        P(("dp", "ep"), None),
        P(("dp", "ep"), None),
        P(("dp", "ep")),
        P(("dp", "ep"), None),
        P(("dp", "ep"), None),
        P("ep", "dp", None),
        P("ep", "dp", None),
        P("ep", "dp", None),
    )
    out_specs = (
        P(("dp", "ep"), None),
        P("ep", "dp", None),
        P("ep", "dp", None),
        P("ep", "dp", None),
    )
    return jax.shard_map(body, mesh=mesh, in_specs=in_specs, out_specs=out_specs, check_vma=False)
```

profile of v0, /device:TPU:1, one launch (start us, length us, event | category | flops | bytes accessed | tf_op | source)
XLA Modules:
  0.0 211.8 jit_solution(488131020382759850)
XLA Ops:
  7.2 0.0 copy-start
  7.2 0.0 all-gather.2.cloned.1.call-start
  7.2 1.7 bitcast_convert_fusion
  9.0 0.0 all-gather.2.cloned.1.call-update
  9.0 69.8 %all-gather.2.cloned.1.call-done = bf16[3584,256]{1,0:T(8,128)(2,1)} async-done(((bf16[224,256]{1,0:T(8,128)(2,1)}), bf16[3584,256]{1,0:T(8,128)(2,1)}) %all-gather.2.cloned.1.call-update) | async-done | bytes 1835024 | tf_op jit(solution)/shard_map/all_gather | solution.py:43
  78.8 3.8 %convolution_convert_fusion = bf16[320,3584]{1,0:T(8,128)(2,1)} fusion(bf16[320,256]{1,0:T(8,128)(2,1)} %param.9, bf16[3584,256]{1,0:T(8,128)(2,1)} %all-gather.2.cloned.1.call-done), kind=kOutput, calls=%fused_computation | convolution fusion | flops 588349440 | bytes 4292608 | tf_op jit(solution)/shard_map/dot_general | solution.py:41
  82.6 4.4 %all_to_all.8 = bf16[32,10,3584]{2,1,0:T(8,128)(2,1)} reshape(bf16[320,3584]{1,0:T(8,128)(2,1)} %convolution_convert_fusion) | data formatting | bytes 4587520 | tf_op jit(solution)/shard_map/all_to_all | solution.py:47
  87.1 0.0 copy-start.7
  87.1 0.0 copy-start.1
  87.1 9.9 %all-to-all-start = ((bf16[32,10,3584]{2,1,0:T(8,128)(2,1)}), bf16[32,10,3584]{2,1,0:T(8,128)(2,1)}, u32[]{:S(2)}, u32[]{:S(2)}) async-start(bf16[32,10,3584]{2,1,0:T(8,128)(2,1)} %all_to_all.8), calls=%async_computation | async-start | bytes 7340032 | tf_op jit(solution)/shard_map/all_to_all | solution.py:47
  97.0 0.0 reduce-scatter.4.cloned.1.call-start
  97.1 0.0 copy-done.7
  97.1 0.1 iota_compare_fusion
  97.1 0.1 lt.39
  97.3 0.0 copy-done
  97.3 0.0 copy-done.1
  97.3 2.5 %fusion = bf16[3584,256]{0,1:T(8,128)(2,1)} fusion(bf16[320,3584]{1,0:T(8,128)(2,1)S(1)} %copy-done, bf16[320,256]{1,0:T(8,128)(2,1)S(1)} %copy-done.1, pred[320]{0:T(512)(128)(4,1)S(1)} %lt.39), kind=kOutput, calls=%fused_computation.2 | convolution fusion | flops 588201984 | bytes 4292928 | tf_op jit(solution)/shard_map/dot_general | solution.py:19
  99.7 0.0 copy-start.5
  99.7 0.0 copy-start.6
  99.7 0.0 copy-start.2
  99.7 0.0 copy-start.3
  99.7 0.0 copy-start.4
  99.8 3.9 %copy.25 = bf16[3584,256]{1,0:T(8,128)(2,1)} copy(bf16[3584,256]{0,1:T(8,128)(2,1)} %fusion) | data formatting | bytes 3670016
  103.7 0.0 reduce-scatter.4.cloned.1.call-update
  103.7 0.0 copy-done.5
  103.8 0.0 copy-done.6
  103.8 90.7 %reduce-scatter.4.cloned.1.call-done = bf16[224,256]{1,0:T(8,128)(2,1)} async-done(((bf16[3584,256]{1,0:T(8,128)(2,1)}), bf16[224,256]{1,0:T(8,128)(2,1)}) %reduce-scatter.4.cloned.1.call-update) | async-done | bytes 114704 | tf_op jit(solution)/shard_map/reduce_scatter | solution.py:18
  194.5 0.0 copy-done.2
  194.5 0.0 copy-done.3
  194.5 0.0 copy-done.4
  194.5 1.9 fusion.34
  196.4 0.0 all-to-all-done
  196.4 4.5 %all_to_all.10 = bf16[320,3584]{1,0:T(8,128)(2,1)} reshape(bf16[32,10,3584]{2,1,0:T(8,128)(2,1)} %all-to-all-done) | data formatting | bytes 4587520 | tf_op jit(solution)/shard_map/all_to_all | solution.py:47
  200.9 4.1 %convolution_convert_fusion.2 = bf16[128,3584]{1,0:T(8,128)(2,1)} fusion(bf16[320,3584]{1,0:T(8,128)(2,1)} %all_to_all.10, s32[128]{0:T(128)S(1)} %get-tuple-element.46, s32[128]{0:T(128)S(1)} %get-tuple-element.29, s32[128]{0:T(128)S(1)} %get-tuple-element.45, s32[128]{0:T(128)S(1)} %get-tuple-element.30, s32[128]{0:T(128)S(1)} %get-tuple-element.51, ...), kind=kOutput, calls=%fused_computation.3 | convolution fusion | flops 295739392 | bytes 3226240 | tf_op jit(solution)/shard_map/dot_general | solution.py:58
  (5 shorter events, 0.0 us)
Async XLA Ops:
  7.2 90.1 %copy-start = (bf16[320,3584]{1,0:T(8,128)(2,1)S(1)}, bf16[320,3584]{1,0:T(8,128)(2,1)}, u32[]{:S(2)}) copy-start(bf16[320,3584]{1,0:T(8,128)(2,1)} %param.8) | copy-start | bytes 6881284
  7.2 71.7 %all-gather.2.cloned.1.call-start = ((), (), s32[]{:S(2)}) async-start(), calls=%async_computation.2 | async-start | bytes 1949696 | tf_op jit(solution)/shard_map/all_gather | solution.py:43
  87.1 10.0 %copy-start.7 = (s32[32]{0:T(128)S(1)}, s32[32]{0:T(128)}, u32[]{:S(2)}) copy-start(s32[32]{0:T(128)} %param.10) | copy-start | bytes 388
  87.1 10.2 %copy-start.1 = (bf16[320,256]{1,0:T(8,128)(2,1)S(1)}, bf16[320,256]{1,0:T(8,128)(2,1)}, u32[]{:S(2)}) copy-start(bf16[320,256]{1,0:T(8,128)(2,1)} %param.9) | copy-start | bytes 491524
  87.1 109.4 %all-to-all-start = ((bf16[32,10,3584]{2,1,0:T(8,128)(2,1)}), bf16[32,10,3584]{2,1,0:T(8,128)(2,1)}, u32[]{:S(2)}, u32[]{:S(2)}) async-start(bf16[32,10,3584]{2,1,0:T(8,128)(2,1)} %all_to_all.8), calls=%async_computation | async-start | bytes 7340032 | tf_op jit(solution)/shard_map/all_to_all | solution.py:47
  97.0 97.5 %reduce-scatter.4.cloned.1.call-start = ((), (), s32[]{:S(2)}) async-start(), calls=%async_computation.3 | async-start | bytes 1949696 | tf_op jit(solution)/shard_map/reduce_scatter | solution.py:18
  99.7 4.0 %copy-start.5 = (s32[128,8]{0,1:T(8,128)S(1)}, s32[128,8]{0,1:T(8,128)}, u32[]{:S(2)}) copy-start(s32[128,8]{0,1:T(8,128)} %param.12) | copy-start | bytes 12292
  99.7 4.0 %copy-start.6 = (s32[128,8]{0,1:T(8,128)S(1)}, s32[128,8]{0,1:T(8,128)}, u32[]{:S(2)}) copy-start(s32[128,8]{0,1:T(8,128)} %param.11) | copy-start | bytes 12292
  99.7 94.8 %copy-start.2 = (f32[1,224,256]{2,1,0:T(8,128)S(1)}, f32[1,224,256]{2,1,0:T(8,128)}, u32[]{:S(2)}) copy-start(f32[1,224,256]{2,1,0:T(8,128)} %param.13) | copy-start | bytes 688132
  99.7 94.8 %copy-start.3 = (f32[1,224,256]{2,1,0:T(8,128)S(1)}, f32[1,224,256]{2,1,0:T(8,128)}, u32[]{:S(2)}) copy-start(f32[1,224,256]{2,1,0:T(8,128)} %param.15) | copy-start | bytes 688132
  99.7 94.8 %copy-start.4 = (f32[1,224,256]{2,1,0:T(8,128)S(1)}, f32[1,224,256]{2,1,0:T(8,128)}, u32[]{:S(2)}) copy-start(f32[1,224,256]{2,1,0:T(8,128)} %param.14) | copy-start | bytes 688132
Sparse Core Ops, SparseCore 0:
  11.6 67.1 all-gather.1
  103.8 90.6 reduce-scatter.3
where the time goes:
time: 213 us; the launch traced here: 212 us
  waiting for transfers between devices  161 us (76%)
  between operations  14.1 us (7%)
  local copies, waits for them, and re-layouts  13 us (6%)
  matrix products  10.3 us (5%)
  starting transfers between devices  10 us (5%)
  other arithmetic  3.77 us (2%)
    reduce_scatter x1, waiting for transfers between devices, update_weights(): lax.psum_scatter(lax.dot_general(expert_inputs, masked_grads, (((0,), (0,...  90.7 us
    all_gather x1, waiting for transfers between devices, return_rows(): lax.all_gather(current_bf, 'dp', axis=0, tiled=True)  69.8 us
    all_to_all x1, starting transfers between devices, return_rows(): lax.all_to_all(partial_rows, 'ep', split_axis=0, concat_axis=0, tiled=True)  9.95 us
    all_to_all x2, local copies, waits for them, and re-layouts, return_rows(): lax.all_to_all(partial_rows, 'ep', split_axis=0, concat_axis=0, tiled=True)  8.88 us
  transfers between devices with their start and end apart: 3, of which 2 were waited for; matrix products, arithmetic and copies ran while one was open for 4% of the time, Pallas kernels for 0%

commit v1 on v0

v1 whole, which is shorter than its diff:
```python
import jax
import jax.numpy as jnp
from jax import lax
from jax.experimental import pallas as pl
from jax.experimental.pallas import tpu as pltpu
from jax.sharding import PartitionSpec as P

MESH = pl.DeviceIdType.MESH
F32 = jnp.float32
BF16 = jnp.bfloat16
I32 = jnp.int32

beta_one = 0.9
beta_two = 0.999
learn_rate = 0.001
adam_epsilon = 1e-08
weight_decay = 0.1
step_count = 100

D = 3584
H = 256
SH = 224
CH = 896
CAP = 10
ROWS = 320
BL = 48
N_SEM = 64


def kernel(
    x_ref, hg_ref, cnt_ref, ids_ref, slots_ref, mw_ref, m1_ref, m2_ref,
    out_ref, nw_ref, n1_ref, n2_ref,
    wown, wbuf, hgp, res, rcv1, rcv2, outg, fin,
    sopp, sside, rx1, rx2, ysopp, ysside, ry1, ry2, gown,
    ssem, rsem,
):
    dp = lax.axis_index("dp")
    ep = lax.axis_index("ep")
    x, y = dp // 4, dp % 4
    yl, z, c = ep // 16, (ep // 2) % 8, ep % 2
    odd = z % 2
    sgn = 2 * odd - 1
    sib = 1 - c
    xs = ((x + 1) % 4, (x + 3) % 4)
    ys = ((y + 1) % 4, (y + 3) % 4)
    x2, y2 = (x + 2) % 4, (y + 2) % 4

    def dev(xx=None, yy=None, ll=None, zz=None, cc=None):
        xx = x if xx is None else xx
        yy = y if yy is None else yy
        ll = yl if ll is None else ll
        zz = z if zz is None else zz
        cc = c if cc is None else cc
        return {"dp": xx * 4 + yy, "ep": ll * 16 + zz * 2 + cc}

    place = {}
    used = [0]

    def sem(name, many=1):
        if name not in place:
            place[name] = used[0]
            used[0] += many
        return place[name]

    def copy(src, dst, at, to, landing=None):
        return pltpu.make_async_remote_copy(
            src_ref=src, dst_ref=dst, send_sem=ssem.at[at], recv_sem=rsem.at[at if landing is None else landing],
            device_id=to, device_id_type=MESH,
        )

    def arrived(dst, at):
        copy(dst, dst, at, dev(cc=sib)).wait_recv()

    def sent(src, at):
        copy(src, src, at, dev(cc=sib)).wait_send()

    def send(src, dst, at, to, landing=None):
        copy(src, dst, at, to, landing).start()

    barrier = pltpu.get_barrier_semaphore()
    near = [dev(cc=sib), dev(xx=xs[0]), dev(xx=xs[1])]
    near += [dev(yy=yy, cc=cc) for yy in ys for cc in (c, sib)]
    near += [dev(zz=(z + t) % 8) for t in (1, 2, 3, 5, 6, 7)]
    near += [dev(ll=1 - yl), dev(ll=1 - yl, cc=sib)]
    for to in near:
        pl.semaphore_signal(barrier, inc=1, device_id=to, device_id_type=MESH)

    wown[...] = mw_ref[...].astype(BF16)
    own_core = x % 2
    is_a = c == own_core
    not_a = c != own_core
    slot_x, slot_o = x // 2, x2 // 2
    slot_s = (xs[0] // 2, xs[1] // 2)

    @pl.when(is_a)
    def _():
        wbuf[slot_x, y, c] = wown[...]

    row = lax.broadcasted_iota(I32, (ROWS, 32), 0)
    blk = lax.broadcasted_iota(I32, (ROWS, 32), 1)
    within = row - CAP * blk
    alive = (within >= 0) & (within < jnp.minimum(cnt_ref[...], CAP))
    alive = jnp.sum(jnp.where(alive, 1.0, 0.0), axis=1, keepdims=True) > 0.5
    masked = jnp.where(alive, hg_ref[...].astype(F32), 0.0).astype(BF16)

    b3 = lax.broadcasted_iota(I32, (8, BL, 1), 0)
    w3 = lax.broadcasted_iota(I32, (8, BL, 1), 1)
    l3 = jnp.where(w3 >= 20, 1, 0)
    u3 = w3 - 20 * l3
    c3 = jnp.where(u3 >= 10, 1, 0)
    p3 = u3 - 10 * c3
    z3 = (jnp.where(b3 < 4, z + sgn * b3, z - sgn * (b3 - 3)) + 16) & 7
    source = jnp.where(w3 < 40, (l3 * 16 + z3 * 2 + c3) * CAP + p3, -1).reshape(8 * BL, 1)
    perm = jnp.where(lax.broadcasted_iota(I32, (8 * BL, ROWS), 1) == source, 1.0, 0.0).astype(BF16)
    hgp[c] = jnp.dot(perm, hg_ref[...], preferred_element_type=F32).astype(BF16)

    def dw_chunk(at):
        cols = pl.ds(pl.multiple_of(at * CH, 128), CH)
        return lax.dot_general(x_ref[:, cols], masked, (((0,), (0,)), ((), ())), preferred_element_type=F32)

    pl.semaphore_wait(barrier, len(near))

    s_wy = [sem("wy_up", 2), sem("wy_down", 2)]
    s_wsib = sem("wsib")
    for k in (0, 1):
        send(wown, wbuf.at[slot_x, y, c], s_wy[k] + c, dev(yy=ys[k], cc=own_core))

    @pl.when(not_a)
    def _():
        send(wown, wbuf.at[slot_x, y, c], s_wsib, dev(cc=sib))

    s_hg = sem("hg")
    send(hgp.at[c], hgp.at[c], s_hg, dev(cc=sib))

    s_rx1 = [sem("rx1_right"), sem("rx1_left")]
    sopp[...] = dw_chunk(x2).astype(BF16).reshape(2, CH // 2, H)
    for k in (0, 1):
        send(sopp.at[k], rx1.at[k], s_rx1[k], dev(xx=xs[k]))
    for k in (0, 1):
        sside[k] = dw_chunk(xs[k]).astype(BF16).reshape(2, CH // 2, H)
    gown[...] = dw_chunk(x).reshape(4, SH, H)

    s_wyf = [sem("wyf_up"), sem("wyf_down")]
    s_wx = [sem("wx_right", 4), sem("wx_left", 4)]
    s_wxf = sem("wxf", 4)
    half = SH // 2
    order = (0, 3, 1, 2)
    forward = (0, 0, 1, 1)

    def yat(d):
        return (y + d) % 4

    def spread(d):
        for k in (0, 1):
            block = wbuf.at[slot_x, yat(d)]
            send(block, block, s_wx[k] + d, dev(xx=xs[k]))

    @pl.when(is_a)
    def _():
        arrived(wbuf.at[slot_x, y, sib], s_wsib)
        spread(0)
        for k, d in ((0, 3), (1, 1)):
            for s in (0, 1):
                arrived(wbuf.at[slot_x, yat(d), s], s_wy[k] + s)
            part = wbuf.at[slot_x, yat(d), :, pl.ds(k * half, half)]
            send(part, part, s_wyf[k], dev(yy=ys[k]))
            spread(d)
        for k in (0, 1):
            arrived(wbuf.at[slot_x, y2, :, pl.ds(k * half, half)], s_wyf[k])
        spread(2)

    @pl.when(not_a)
    def _():
        for d in order:
            for k in (0, 1):
                block = wbuf.at[slot_s[1 - k], yat(d)]
                arrived(block, s_wx[k] + d)
                if forward[d] == k:
                    send(block, block, s_wxf + d, dev(xx=xs[k]))

    first = jnp.where(is_a, slot_x, slot_s[1])
    chunk = (2 * first + c, 2 * (1 - first) + c)
    slot = (first, 1 - first)
    arrived(hgp.at[sib], s_hg)

    s_r1 = sem("rows1", 2)
    s_r2 = sem("rows2", 8)
    s_fin = sem("fin", 8)

    def rows_one(i):
        total = jnp.zeros((8 * BL, CH), F32)
        for s in (0, 1):
            total += lax.dot_general(
                hgp[s], wbuf[slot[i], :, s].reshape(CH, H), (((1,), (1,)), ((), ())), preferred_element_type=F32
            )
        res[i] = total.astype(BF16).reshape(8, BL, CH)
        send(res.at[i, pl.ds(4, 4)], rcv1.at[i], s_r1 + i, dev(zz=(z - sgn + 8) % 8))

    def rows_two(i):
        arrived(rcv1.at[i], s_r1 + i)
        for t in (3, 2, 1, 0):
            both = (res[i, t].astype(F32) + rcv1[i, t].astype(F32)).astype(BF16)
            if t == 0:
                rcv2[i, 0] = both
            else:
                res[i, t] = both
                send(res.at[i, t], rcv2.at[i, t], s_r2 + 4 * i + t, dev(zz=(z + sgn * t + 8) % 8))

    rr = lax.broadcasted_iota(I32, (128, 4 * BL), 0)
    col = lax.broadcasted_iota(I32, (1, 4 * BL), 1)
    tt = jnp.zeros_like(col)
    for t in (1, 2, 3):
        tt = tt + jnp.where(col >= t * BL, 1, 0)
    ww = col - BL * tt
    gg = jnp.zeros_like(col)
    for g in (1, 2, 3):
        gg = gg + jnp.where(ww >= g * CAP, 1, 0)
    expert = jnp.zeros_like(col)
    for t in range(4):
        step = -sgn * t if t % 2 == 0 else sgn * t
        expert = jnp.where(tt == t, ((z + step + 8) % 8) // 4, expert)
    target = jnp.where(ww < 40, gg * 32 + expert * CAP + ww - CAP * gg, -1)
    sorting = jnp.where(rr == target, 1.0, 0.0).astype(BF16)
    owners = ((1 - yl, c), (1 - yl, sib), (yl, sib))

    def rows_three(i):
        for t in (1, 2, 3):
            arrived(rcv2.at[i, t], s_r2 + 4 * i + t)
        rows = jnp.dot(sorting, rcv2[i].reshape(4 * BL, CH), preferred_element_type=F32)
        outg[i] = rows.astype(BF16).reshape(4, 32, CH)
        for k, (ll, cc) in enumerate(owners):
            send(outg.at[i, ll * 2 + cc], fin.at[chunk[i], yl], s_fin + 3 * i + k, dev(ll=ll, cc=cc),
                 s_fin + 2 * chunk[i] + yl)
        fin[chunk[i], yl] = outg[i, yl * 2 + c]

    s_rx2 = [sem("rx2_right"), sem("rx2_left")]
    s_ry1 = [sem("ry1_up"), sem("ry1_down")]
    s_ry2 = [sem("ry2_up"), sem("ry2_down")]

    def grads_two():
        for k in (0, 1):
            arrived(rx1.at[k], s_rx1[k])
            sside[k, k] = (sside[k, k].astype(F32) + rx1[k].astype(F32)).astype(BF16)
            send(sside.at[k], rx2.at[k], s_rx2[k], dev(xx=xs[k]))

    def grads_three():
        for k in (0, 1):
            arrived(rx2.at[k], s_rx2[k])

        def over_x(at):
            rows = gown[at]
            for k in (0, 1):
                rows = rows + rx2[k, at // 2, pl.ds(pl.multiple_of((at % 2) * SH, 16), SH)].astype(F32)
            return rows

        ysopp[...] = over_x(y2).astype(BF16).reshape(2, SH // 2, H)
        for k in (0, 1):
            send(ysopp.at[k], ry1.at[k], s_ry1[k], dev(yy=ys[k]))
        for k in (0, 1):
            ysside[k] = over_x(ys[k]).astype(BF16).reshape(2, SH // 2, H)
        gown[y] = over_x(y)

    def grads_four():
        for k in (0, 1):
            arrived(ry1.at[k], s_ry1[k])
            ysside[k, k] = (ysside[k, k].astype(F32) + ry1[k].astype(F32)).astype(BF16)
            send(ysside.at[k], ry2.at[k], s_ry2[k], dev(yy=ys[k]))

    def adam():
        for k in (0, 1):
            arrived(ry2.at[k], s_ry2[k])
        grads = gown[y] + ry2[0].reshape(SH, H).astype(F32) + ry2[1].reshape(SH, H).astype(F32)
        master = mw_ref[...]
        new_first = beta_one * m1_ref[...] + (1.0 - beta_one) * grads
        new_second = beta_two * m2_ref[...] + (1.0 - beta_two) * grads * grads
        first_hat = new_first / (1.0 - beta_one**step_count)
        second_hat = new_second / (1.0 - beta_two**step_count)
        nw_ref[...] = master - learn_rate * (
            first_hat / (jnp.sqrt(second_hat) + adam_epsilon) + weight_decay * master
        )
        n1_ref[...] = new_first
        n2_ref[...] = new_second

    rows_one(0)
    grads_two()
    rows_two(0)

    @pl.when(is_a)
    def _():
        for d in order:
            arrived(wbuf.at[slot_o, yat(d)], s_wxf + d)

    rows_one(1)
    grads_three()
    rows_three(0)
    rows_two(1)
    grads_four()
    rows_three(1)
    adam()

    wanted = lax.broadcasted_iota(I32, (64, 128), 0)
    table = jnp.zeros((64, 128), F32)
    for r in range(ids_ref.shape[0]):
        expert_id = ids_ref[pl.ds(r, 1), :]
        slot_id = slots_ref[pl.ds(r, 1), :]
        lower = jnp.where(expert_id >= 2, 1, 0)
        code = lower * 32 + (expert_id - 2 * lower) * CAP + slot_id
        code = jnp.where((slot_id >= 0) & (expert_id < 4), code, -1)
        table = table + jnp.where(wanted == code, 1.0, 0.0)
    table = table.astype(BF16)

    for at in range(4):
        arrived(fin.at[at, 1 - yl], s_fin + 2 * at + 1 - yl)

        @pl.when(c != at % 2)
        def _():
            arrived(fin.at[at, yl], s_fin + 2 * at + yl)

        out_ref[:, pl.ds(at * CH, CH)] = lax.dot_general(
            table, fin[at].reshape(64, CH), (((0,), (0,)), ((), ())), preferred_element_type=F32
        ).astype(BF16)

    for k in (0, 1):
        sent(wown, s_wy[k] + c)
        sent(sopp.at[k], s_rx1[k])
        sent(sside.at[k], s_rx2[k])
        sent(ysopp.at[k], s_ry1[k])
        sent(ysside.at[k], s_ry2[k])
        sent(res.at[k, pl.ds(4, 4)], s_r1 + k)
        for t in (1, 2, 3):
            sent(res.at[k, t], s_r2 + 4 * k + t)
            sent(outg.at[k, t], s_fin + 3 * k + t - 1)
    sent(hgp.at[c], s_hg)

    @pl.when(is_a)
    def _():
        for k, d in ((0, 3), (1, 1)):
            sent(wbuf.at[slot_x, yat(d), :, pl.ds(k * half, half)], s_wyf[k])
        for d in order:
            for k in (0, 1):
                sent(wbuf.at[slot_x, yat(d)], s_wx[k] + d)

    @pl.when(not_a)
    def _():
        sent(wown, s_wsib)
        for d in order:
            sent(wbuf.at[slot_s[1 - forward[d]], yat(d)], s_wxf + d)


def body(expert_inputs, hidden_grads, row_counts, top_ids, route_slots, master, first, second):
    vmem = pl.BlockSpec(memory_space=pltpu.VMEM)
    shard = jax.ShapeDtypeStruct((SH, H), F32)
    out, new_master, new_first, new_second = pl.pallas_call(
        kernel,
        out_shape=(jax.ShapeDtypeStruct((128, D), BF16), shard, shard, shard),
        in_specs=[vmem] * 8,
        out_specs=(vmem,) * 4,
        scratch_shapes=[
            pltpu.VMEM((SH, H), BF16),
            pltpu.VMEM((2, 4, 2, SH, H), BF16),
            pltpu.VMEM((2, 8 * BL, H), BF16),
            pltpu.VMEM((2, 8, BL, CH), BF16),
            pltpu.VMEM((2, 4, BL, CH), BF16),
            pltpu.VMEM((2, 4, BL, CH), BF16),
            pltpu.VMEM((2, 4, 32, CH), BF16),
            pltpu.VMEM((4, 2, 32, CH), BF16),
            pltpu.VMEM((2, CH // 2, H), BF16),
            pltpu.VMEM((2, 2, CH // 2, H), BF16),
            pltpu.VMEM((2, CH // 2, H), BF16),
            pltpu.VMEM((2, 2, CH // 2, H), BF16),
            pltpu.VMEM((2, SH // 2, H), BF16),
            pltpu.VMEM((2, 2, SH // 2, H), BF16),
            pltpu.VMEM((2, SH // 2, H), BF16),
            pltpu.VMEM((2, 2, SH // 2, H), BF16),
            pltpu.VMEM((4, SH, H), F32),
            pltpu.SemaphoreType.DMA((N_SEM,)),
            pltpu.SemaphoreType.DMA((N_SEM,)),
        ],
        compiler_params=pltpu.CompilerParams(
            collective_id=0, has_side_effects=True, vmem_limit_bytes=48 * 2**20
        ),
    )(
        expert_inputs, hidden_grads, row_counts.reshape(1, 32), top_ids.T, route_slots.T,
        master[0], first[0], second[0],
    )
    return out, new_master[None], new_first[None], new_second[None]


def solution(mesh):
    rows = P(("dp", "ep"), None)
    weights = P("ep", "dp", None)
    return jax.shard_map(
        body,
        mesh=mesh,
        in_specs=(rows, rows, P(("dp", "ep")), rows, rows, weights, weights, weights),
        out_specs=(rows, weights, weights, weights),
        check_vma=False,
    )
```

time: 213 us -> 80.1 us (0.38)
  waiting for transfers between devices: 161 us -> 0 us
  Pallas kernels: 0 us -> 68.7 us
  between operations: 14.1 us -> 0.66 us
  matrix products: 10.3 us -> 0 us
  starting transfers between devices: 10 us -> 0 us
  other arithmetic: 3.77 us -> 0 us
  local copies, waits for them, and re-layouts: 13 us -> 10.4 us
    reduce_scatter x1 -> x0, waiting for transfers between devices: 90.7 us -> none  [update_weights(): lax.psum_scatter(lax.dot_general(expert_inputs, masked_grads, (((0,), (0,...]
    all_gather x1 -> x0, waiting for transfers between devices: 69.8 us -> none  [return_rows(): lax.all_gather(current_bf, 'dp', axis=0, tiled=True)]
    pallas_call x0 -> x1, Pallas kernels: none -> 68.7 us  [body(): pl.pallas_call(kernel, out_shape=(jax.ShapeDtypeStruct((128, D), BF16), s...]
    dot_general x3 -> x0, matrix products: 10.3 us -> none  [the longest x1 4.09 us: return_rows(): jnp.dot(combine_table, received, preferred_element_type=jnp.float32)]
    all_to_all x1 -> x0, starting transfers between devices: 9.95 us -> none  [return_rows(): lax.all_to_all(partial_rows, 'ep', split_axis=0, concat_axis=0, tiled=True)]
    all_to_all x2 -> x0, local copies, waits for them, and re-layouts: 8.88 us -> none  [return_rows(): lax.all_to_all(partial_rows, 'ep', split_axis=0, concat_axis=0, tiled=True)]
    unnamed x17 -> x20, local copies, waits for them, and re-layouts: 3.96 us -> 10.4 us
  transfers between devices with their start and end apart: 3 -> 0, of which waited for: 2 -> 0; matrix products, arithmetic and copies ran while one was open for 4% -> 0% of each run, Pallas kernels for 0% -> 0%
where the time goes in v1:
time: 80.1 us; the launch traced here: 79.8 us
  Pallas kernels  68.7 us (86%)
  local copies, waits for them, and re-layouts  10.4 us (13%)
    pallas_call x1, Pallas kernels, body(): pl.pallas_call(kernel, out_shape=(jax.ShapeDtypeStruct((128, D), BF16), s...  68.7 us
    unnamed x20, local copies, waits for them, and re-layouts  10.4 us

profile of v1, /device:TPU:1, one launch (start us, length us, event | category | flops | bytes accessed | tf_op | source)
XLA Modules:
  0.0 79.8 jit_solution(10187985934320151920)
XLA Ops:
  0.6 0.0 copy-start
  0.6 1.6 %copy-done = bf16[320,3584]{1,0:T(8,128)(2,1)S(1)} copy-done((bf16[320,3584]{1,0:T(8,128)(2,1)S(1)}, bf16[320,3584]{1,0:T(8,128)(2,1)}, u32[]{:S(2)}) %copy-start) | copy-done | bytes 2293784
  2.3 0.0 copy-start.1
  2.3 0.9 %copy-done.1 = f32[1,224,256]{2,1,0:T(8,128)S(1)} copy-done((f32[1,224,256]{2,1,0:T(8,128)S(1)}, f32[1,224,256]{2,1,0:T(8,128)}, u32[]{:S(2)}) %copy-start.1) | copy-done | bytes 229400
  3.2 0.0 copy-start.2
  3.2 0.9 %copy-done.2 = f32[1,224,256]{2,1,0:T(8,128)S(1)} copy-done((f32[1,224,256]{2,1,0:T(8,128)S(1)}, f32[1,224,256]{2,1,0:T(8,128)}, u32[]{:S(2)}) %copy-start.2) | copy-done | bytes 229400
  4.2 0.0 copy-start.3
  4.2 0.9 %copy-done.3 = f32[1,224,256]{2,1,0:T(8,128)S(1)} copy-done((f32[1,224,256]{2,1,0:T(8,128)S(1)}, f32[1,224,256]{2,1,0:T(8,128)}, u32[]{:S(2)}) %copy-start.3) | copy-done | bytes 229400
  5.1 0.0 copy-start.4
  5.1 0.9 %copy-done.4 = bf16[320,256]{1,0:T(8,128)(2,1)S(1)} copy-done((bf16[320,256]{1,0:T(8,128)(2,1)S(1)}, bf16[320,256]{1,0:T(8,128)(2,1)}, u32[]{:S(2)}) %copy-start.4) | copy-done | bytes 163864
  6.0 0.0 copy-start.5
  6.0 0.7 copy-done.5
  6.7 0.0 copy-start.6
  6.7 0.7 copy-done.6
  7.4 0.0 copy-start.7
  7.4 0.7 copy-done.7
  8.0 68.7 %shard_map.111 = (bf16[128,3584]{1,0:T(8,128)(2,1)S(1)}, f32[224,256]{1,0:T(8,128)S(1)}, f32[224,256]{1,0:T(8,128)S(1)}, f32[224,256]{1,0:T(8,128)S(1)}) custom-call(bf16[320,3584]{1,0:T(8,128)(2,1)S(1)} %copy-done, bf16[320,256]{1,0:T(8,128)(2,1)S(1)} %copy-done.4, s32[1,32]{1,0:T(1,128)S(1)} %bitcast.17, s32[8,128]{1,0:T(8,128)S(1)} %bitcast.15, ...), custom_call_target="tpu_custom_call" | custom-call | tf_op jit(solution)/shard_map/pallas_call | solution.py:353
  76.8 0.9 %copy.16 = bf16[128,3584]{1,0:T(8,128)(2,1)} copy(bf16[128,3584]{1,0:T(8,128)(2,1)S(1)} %get-tuple-element.16) | data formatting | bytes 1835008
  77.7 0.7 copy.17
  78.4 0.7 copy.18
  79.1 0.7 copy.19
Async XLA Ops:
  0.6 1.6 %copy-start = (bf16[320,3584]{1,0:T(8,128)(2,1)S(1)}, bf16[320,3584]{1,0:T(8,128)(2,1)}, u32[]{:S(2)}) copy-start(bf16[320,3584]{1,0:T(8,128)(2,1)} %x_ref.1) | copy-start | bytes 6881284
  2.3 0.9 %copy-start.1 = (f32[1,224,256]{2,1,0:T(8,128)S(1)}, f32[1,224,256]{2,1,0:T(8,128)}, u32[]{:S(2)}) copy-start(f32[1,224,256]{2,1,0:T(8,128)} %param.13) | copy-start | bytes 688132
  3.2 0.9 %copy-start.2 = (f32[1,224,256]{2,1,0:T(8,128)S(1)}, f32[1,224,256]{2,1,0:T(8,128)}, u32[]{:S(2)}) copy-start(f32[1,224,256]{2,1,0:T(8,128)} %param.14) | copy-start | bytes 688132
  4.2 0.9 %copy-start.3 = (f32[1,224,256]{2,1,0:T(8,128)S(1)}, f32[1,224,256]{2,1,0:T(8,128)}, u32[]{:S(2)}) copy-start(f32[1,224,256]{2,1,0:T(8,128)} %param.15) | copy-start | bytes 688132
  5.1 0.9 %copy-start.4 = (bf16[320,256]{1,0:T(8,128)(2,1)S(1)}, bf16[320,256]{1,0:T(8,128)(2,1)}, u32[]{:S(2)}) copy-start(bf16[320,256]{1,0:T(8,128)(2,1)} %hg_ref.1) | copy-start | bytes 491524
  6.0 0.7 copy-start.5
  6.7 0.7 copy-start.6
  7.4 0.7 copy-start.7

commit v2 on v1

v2 whole, which is shorter than its diff:
```python
import jax
import jax.numpy as jnp
from jax import lax
from jax.experimental import pallas as pl
from jax.experimental.pallas import tpu as pltpu
from jax.sharding import PartitionSpec as P

MESH = pl.DeviceIdType.MESH
F32 = jnp.float32
BF16 = jnp.bfloat16
I32 = jnp.int32

beta_one = 0.9
beta_two = 0.999
learn_rate = 0.001
adam_epsilon = 1e-08
weight_decay = 0.1
step_count = 100

D = 3584
H = 256
SH = 224
CH = 896
CAP = 10
ROWS = 320
BL = 80
N_SEM = 128
UNITS = (((0, 0, 224), (1, 0, 208), (3, 0, 208)), ((1, 208, 16), (3, 208, 16), (2, 0, 224)))
WIDTHS = tuple(sum(n for _, _, n in unit) for unit in UNITS)
PLACES = (0, WIDTHS[0])


def kernel(
    x_hbm, hg_hbm, cnt_hbm, ids_hbm, slots_hbm, mw_hbm, m1_hbm, m2_hbm,
    out_ref, nw_ref, n1_ref, n2_ref,
    x_ref, hg_ref, cnt_ref, ids_ref, slots_ref, mw_ref, m1_ref, m2_ref,
    wown, wbuf, hgall, hgp, place, sopp, sside, rx1, rx2, ysopp, ysside, ry1, ry2, gown,
    ssem, rsem, lsem, *by_unit,
):
    n_units = len(UNITS)
    res, rcv1, rcv2, outg, fin = (by_unit[n_units * n : n_units * (n + 1)] for n in range(5))

    dp = lax.axis_index("dp")
    ep = lax.axis_index("ep")
    x, y = dp // 4, dp % 4
    yl, z, c = ep // 16, (ep // 2) % 8, ep % 2
    odd = z % 2
    sgn = 2 * odd - 1
    sib = 1 - c
    xs = ((x + 1) % 4, (x + 3) % 4)
    ys = ((y + 1) % 4, (y + 3) % 4)
    x2, y2 = (x + 2) % 4, (y + 2) % 4
    xp = x + 1 - 2 * (x % 2)
    xw = 3 - x

    def dev(xx=None, yy=None, ll=None, zz=None, cc=None):
        xx = x if xx is None else xx
        yy = y if yy is None else yy
        ll = yl if ll is None else ll
        zz = z if zz is None else zz
        cc = c if cc is None else cc
        return {"dp": xx * 4 + yy, "ep": ll * 16 + zz * 2 + cc}

    spots = {}
    used = [0]

    def sem(name, many=1):
        if name not in spots:
            spots[name] = used[0]
            used[0] += many
        return spots[name]

    def copy(src, dst, at, to, landing=None):
        return pltpu.make_async_remote_copy(
            src_ref=src, dst_ref=dst, send_sem=ssem.at[at], recv_sem=rsem.at[at if landing is None else landing],
            device_id=to, device_id_type=MESH,
        )

    def arrived(dst, at):
        copy(dst, dst, at, dev(cc=sib)).wait_recv()

    def sent(src, at):
        copy(src, src, at, dev(cc=sib)).wait_send()

    def send(src, dst, at, to, landing=None):
        copy(src, dst, at, to, landing).start()

    barrier = pltpu.get_barrier_semaphore()
    near = [dev(cc=sib), dev(xx=xs[0]), dev(xx=xs[1])]
    near += [dev(yy=yy, cc=cc) for yy in ys for cc in (c, sib)]
    near += [dev(zz=(z + t) % 8) for t in (1, 2, 3, 5, 6, 7)]
    near += [dev(xx=xp, cc=sib), dev(xx=xw, cc=sib)]
    near += [dev(xx=xx, ll=1 - yl, cc=cc) for xx in (x, xp) for cc in (c, sib)]
    for to in near:
        pl.semaphore_signal(barrier, inc=1, device_id=to, device_id_type=MESH)

    loads = {}
    pairs = (
        ("mw", mw_hbm, mw_ref), ("hg", hg_hbm, hg_ref), ("cnt", cnt_hbm, cnt_ref), ("x", x_hbm, x_ref),
        ("ids", ids_hbm, ids_ref), ("slots", slots_hbm, slots_ref), ("m1", m1_hbm, m1_ref), ("m2", m2_hbm, m2_ref),
    )
    for n, (name, there, here) in enumerate(pairs):
        loads[name] = pltpu.make_async_copy(there, here, lsem.at[n])
        loads[name].start()

    loads["mw"].wait()
    wown[...] = mw_ref[...].astype(BF16)
    is_a = c == 0
    not_a = c == 1

    @pl.when(is_a)
    def _():
        wbuf[y, c] = wown[...]

    def dw_chunk(at):
        cols = pl.ds(pl.multiple_of(at * CH, 128), CH)
        return lax.dot_general(x_ref[:, cols], masked, (((0,), (0,)), ((), ())), preferred_element_type=F32)

    pl.semaphore_wait(barrier, len(near))

    s_wy = [sem("wy_up", 2), sem("wy_down", 2)]
    s_wsib = sem("wsib")
    for k in (0, 1):
        send(wown, wbuf.at[y, c], s_wy[k] + c, dev(yy=ys[k], cc=0))

    @pl.when(not_a)
    def _():
        send(wown, wbuf.at[y, c], s_wsib, dev(cc=sib))

    loads["hg"].wait()
    s_hg = sem("hg", 3)
    hgall[0, c] = hg_ref[...]
    send(hgall.at[0, c], hgall.at[1, c], s_hg, dev(xx=xp))
    send(hgall.at[0, c], hgall.at[0, c], s_hg + 1, dev(cc=sib))
    loads["cnt"].wait()

    row = lax.broadcasted_iota(I32, (ROWS, 32), 0)
    blk = lax.broadcasted_iota(I32, (ROWS, 32), 1)
    within = row - CAP * blk
    alive = (within >= 0) & (within < jnp.minimum(cnt_ref[...], CAP))
    alive = jnp.sum(jnp.where(alive, 1.0, 0.0), axis=1, keepdims=True) > 0.5
    masked = jnp.where(alive, hg_ref[...].astype(F32), 0.0).astype(BF16)

    b3 = lax.broadcasted_iota(I32, (8, BL, 1), 0)
    w3 = lax.broadcasted_iota(I32, (8, BL, 1), 1)
    r3 = jnp.where(w3 >= 40, 1, 0)
    v3 = w3 - 40 * r3
    l3 = jnp.where(v3 >= 20, 1, 0)
    u3 = v3 - 20 * l3
    c3 = jnp.where(u3 >= 10, 1, 0)
    p3 = u3 - 10 * c3
    z3 = (jnp.where(b3 < 4, z + sgn * b3, z - sgn * (b3 - 3)) + 16) & 7
    source = (r3 * ROWS + (l3 * 16 + z3 * 2 + c3) * CAP + p3).reshape(8 * BL, 1)
    perm = jnp.where(lax.broadcasted_iota(I32, (8 * BL, 2 * ROWS), 1) == source, 1.0, 0.0).astype(BF16)

    loads["x"].wait()
    part = SH // 2
    s_rx1 = [sem("rx1_right", 4), sem("rx1_left", 4)]
    s_rx2 = [sem("rx2_right", 4), sem("rx2_left", 4)]
    s_ry1 = [sem("ry1_up"), sem("ry1_down")]
    s_ry2 = [sem("ry2_up"), sem("ry2_down")]
    far_first = (2, 1, 3, 0)

    def yat(d):
        return (y + d) % 4

    sopp[...] = dw_chunk(x2).astype(BF16).reshape(4, 2, part, H)

    def grads_one():
        for d in far_first:
            for k in (0, 1):
                send(sopp.at[yat(d), k], rx1.at[k, yat(d)], s_rx1[k] + d, dev(xx=xs[k]))

    for k in (0, 1):
        sside[k] = dw_chunk(xs[k]).astype(BF16).reshape(4, 2, part, H)
    gown[...] = dw_chunk(x).reshape(4, SH, H)

    s_wyf = [sem("wyf_up"), sem("wyf_down")]
    s_wx = sem("wx", 4)
    order = (0, 3, 1, 2)

    def half_of(d, k):
        return wbuf.at[yat(d), :, pl.ds(k * part, part)]

    def spread(d):
        send(wbuf.at[yat(d)], wbuf.at[yat(d)], s_wx + d, dev(xx=xw, cc=sib))

    def gather_a():
        arrived(wbuf.at[y, sib], s_wsib)
        spread(0)
        for k, d in ((0, 3), (1, 1)):
            for s in (0, 1):
                arrived(wbuf.at[yat(d), s], s_wy[k] + s)
            send(half_of(d, k), half_of(d, k), s_wyf[k], dev(yy=ys[k]))
            spread(d)

    def gather_a_last():
        for k in (0, 1):
            arrived(half_of(2, k), s_wyf[k])
        spread(2)

    def gather_b():
        for d in (0, 3, 1):
            arrived(wbuf.at[yat(d)], s_wx + d)

    def gather_b_last():
        arrived(wbuf.at[y2], s_wx + 2)

    def rows_in():
        arrived(hgall.at[1, c], s_hg)
        send(hgall.at[1, c], hgall.at[1, c], s_hg + 2, dev(cc=sib))
        arrived(hgall.at[0, sib], s_hg + 1)
        arrived(hgall.at[1, sib], s_hg + 2)
        for s in (0, 1):
            both = jnp.concatenate([hgall[0, s], hgall[1, s]], axis=0)
            hgp[s] = jnp.dot(perm, both, preferred_element_type=F32).astype(BF16)

    n_units = len(UNITS)
    s_r1 = sem("rows1", n_units)
    s_r2 = sem("rows2", 4 * n_units)
    s_fin = sem("fin", 8 * n_units)

    def rows_one(u):
        total = jnp.zeros((8 * BL, WIDTHS[u]), F32)
        for s in (0, 1):
            weights = jnp.concatenate([wbuf[yat(d), s, pl.ds(at, n)] for d, at, n in UNITS[u]], axis=0)
            total += lax.dot_general(hgp[s], weights, (((1,), (1,)), ((), ())), preferred_element_type=F32)
        res[u][...] = total.astype(BF16).reshape(2, 4 * BL, WIDTHS[u])
        send(res[u].at[1], rcv1[u], s_r1 + u, dev(zz=(z - sgn + 8) % 8))

    def rows_two(u):
        arrived(rcv1[u], s_r1 + u)
        res[u][0] = (res[u][0].astype(F32) + rcv1[u][...].astype(F32)).astype(BF16)
        for t in (3, 2, 1):
            send(res[u].at[0, pl.ds(t * BL, BL)], rcv2[u].at[t], s_r2 + 4 * u + t, dev(zz=(z + sgn * t + 8) % 8))
        rcv2[u][0] = res[u][0, pl.ds(0, BL)]

    rr = lax.broadcasted_iota(I32, (256, 4 * BL), 0)
    col = lax.broadcasted_iota(I32, (1, 4 * BL), 1)
    tt = jnp.zeros_like(col)
    for t in (1, 2, 3):
        tt = tt + jnp.where(col >= t * BL, 1, 0)
    ww = col - BL * tt
    gg = jnp.zeros_like(col)
    for g in range(1, 8):
        gg = gg + jnp.where(ww >= g * CAP, 1, 0)
    expert = jnp.zeros_like(col)
    for t in range(4):
        step = -sgn * t if t % 2 == 0 else sgn * t
        expert = jnp.where(tt == t, ((z + step + 8) % 8) // 4, expert)
    target = gg * 32 + expert * CAP + ww - CAP * gg
    sorting = jnp.where(rr == target, 1.0, 0.0).astype(BF16)
    owners = [(rep, ll, cc) for rep in (1, 0) for ll in (1 - yl, yl) for cc in (c, sib)]

    def rows_three(u):
        for t in (1, 2, 3):
            arrived(rcv2[u].at[t], s_r2 + 4 * u + t)
        rows = jnp.dot(sorting, rcv2[u][...].reshape(4 * BL, WIDTHS[u]), preferred_element_type=F32)
        outg[u][...] = rows.astype(BF16).reshape(8, 32, WIDTHS[u])
        for k, (rep, ll, cc) in enumerate(owners):
            if k == 6:
                fin[u][0, c, yl] = outg[u][yl * 2 + c]
                continue
            send(outg[u].at[rep * 4 + ll * 2 + cc], fin[u].at[rep, c, yl], s_fin + 8 * u + k,
                 dev(xx=(x, xp)[rep], ll=ll, cc=cc), s_fin + 8 * u + 4 * rep + 2 * c + yl)

    def grads_two():
        for d in far_first:
            for k in (0, 1):
                arrived(rx1.at[k, yat(d)], s_rx1[k] + d)
                sside[k, yat(d), k] = (sside[k, yat(d), k].astype(F32) + rx1[k, yat(d)].astype(F32)).astype(BF16)
                send(sside.at[k, yat(d)], rx2.at[k, yat(d)], s_rx2[k] + d, dev(xx=xs[k]))

    def over_x(d):
        rows = gown[yat(d)]
        for k in (0, 1):
            arrived(rx2.at[k, yat(d)], s_rx2[k] + d)
            rows = rows + rx2[k, yat(d)].reshape(SH, H).astype(F32)
        return rows

    def grads_three():
        ysopp[...] = over_x(2).astype(BF16).reshape(2, part, H)
        for k in (0, 1):
            send(ysopp.at[k], ry1.at[k], s_ry1[k], dev(yy=ys[k]))

    def grads_four():
        for k, d in ((0, 1), (1, 3)):
            rows = over_x(d).reshape(2, part, H)
            arrived(ry1.at[k], s_ry1[k])
            ysside[k, k] = (rows[k] + ry1[k].astype(F32)).astype(BF16)
            ysside[k, 1 - k] = rows[1 - k].astype(BF16)
            send(ysside.at[k], ry2.at[k], s_ry2[k], dev(yy=ys[k]))

    def adam():
        grads = over_x(0)
        for k in (0, 1):
            arrived(ry2.at[k], s_ry2[k])
        for name in ("m1", "m2"):
            loads[name].wait()
        grads = grads + ry2[0].reshape(SH, H).astype(F32) + ry2[1].reshape(SH, H).astype(F32)
        master = mw_ref[...]
        new_first = beta_one * m1_ref[...] + (1.0 - beta_one) * grads
        new_second = beta_two * m2_ref[...] + (1.0 - beta_two) * grads * grads
        first_hat = new_first / (1.0 - beta_one**step_count)
        second_hat = new_second / (1.0 - beta_two**step_count)
        nw_ref[...] = master - learn_rate * (
            first_hat / (jnp.sqrt(second_hat) + adam_epsilon) + weight_decay * master
        )
        n1_ref[...] = new_first
        n2_ref[...] = new_second

    from_col = lax.broadcasted_iota(I32, (CH, 1), 0)
    belongs = jnp.zeros_like(from_col)
    done = 0
    for unit in UNITS:
        for d, at, n in unit:
            belongs = jnp.where(from_col >= done, yat(d) * SH + at + from_col - done, belongs)
            done += n
    place[...] = jnp.where(lax.broadcasted_iota(I32, (CH, CH), 1) == belongs, 1.0, 0.0).astype(BF16)

    @pl.when(is_a)
    def _():
        gather_a()
        grads_one()
        rows_in()
        rows_one(0)
        gather_a_last()
        rows_one(1)
        grads_two()
        rows_two(0)

    @pl.when(not_a)
    def _():
        grads_one()
        rows_in()
        gather_b()
        rows_one(0)
        grads_two()
        gather_b_last()
        rows_one(1)
        rows_two(0)

    rows_two(1)
    grads_three()
    rows_three(0)
    grads_four()
    rows_three(1)
    adam()

    wanted = lax.broadcasted_iota(I32, (64, 128), 0)
    table = jnp.zeros((64, 128), F32)
    loads["ids"].wait()
    loads["slots"].wait()
    for r in range(ids_ref.shape[0]):
        expert_id = ids_ref[pl.ds(r, 1), :]
        slot_id = slots_ref[pl.ds(r, 1), :]
        lower = jnp.where(expert_id >= 2, 1, 0)
        code = lower * 32 + (expert_id - 2 * lower) * CAP + slot_id
        code = jnp.where((slot_id >= 0) & (expert_id < 4), code, -1)
        table = table + jnp.where(wanted == code, 1.0, 0.0)
    table = table.astype(BF16)

    for u in range(n_units):
        for rep in (0, 1):
            for ll in (yl, 1 - yl):
                for cc in (c, sib):
                    if rep == 1 or ll is not yl or cc is not c:
                        arrived(fin[u].at[rep, cc, ll], s_fin + 8 * u + 4 * rep + 2 * cc + ll)
    for rep in (0, 1):
        for cc in (0, 1):
            natural = jnp.zeros((64, CH), F32)
            for u in range(n_units):
                natural += jnp.dot(
                    fin[u][rep, cc].reshape(64, WIDTHS[u]), place[pl.ds(PLACES[u], WIDTHS[u])],
                    preferred_element_type=F32,
                )
            from_x = (x, xp)[rep]
            chunk = (from_x, 3 - from_x)[cc]
            out_ref[:, pl.ds(pl.multiple_of(chunk * CH, 128), CH)] = lax.dot_general(
                table, natural.astype(BF16), (((0,), (0,)), ((), ())), preferred_element_type=F32
            ).astype(BF16)

    for k in (0, 1):
        sent(wown, s_wy[k] + c)
        for d in order:
            sent(sopp.at[yat(d), k], s_rx1[k] + d)
            sent(sside.at[k, yat(d)], s_rx2[k] + d)
        sent(ysopp.at[k], s_ry1[k])
        sent(ysside.at[k], s_ry2[k])
    for u in range(n_units):
        sent(res[u].at[1], s_r1 + u)
        for t in (1, 2, 3):
            sent(res[u].at[0, pl.ds(t * BL, BL)], s_r2 + 4 * u + t)
        for k in (0, 1, 2, 3, 4, 5, 7):
            sent(outg[u].at[k], s_fin + 8 * u + k)
    for k in (0, 1):
        sent(hgall.at[0, c], s_hg + k)
    sent(hgall.at[1, c], s_hg + 2)

    @pl.when(is_a)
    def _():
        for k, d in ((0, 3), (1, 1)):
            sent(half_of(d, k), s_wyf[k])
        for d in order:
            sent(wbuf.at[yat(d)], s_wx + d)

    @pl.when(not_a)
    def _():
        sent(wown, s_wsib)


def body(expert_inputs, hidden_grads, row_counts, top_ids, route_slots, master, first, second):
    vmem = pl.BlockSpec(memory_space=pltpu.VMEM)
    shard = jax.ShapeDtypeStruct((SH, H), F32)
    out, new_master, new_first, new_second = pl.pallas_call(
        kernel,
        out_shape=(jax.ShapeDtypeStruct((128, D), BF16), shard, shard, shard),
        in_specs=[pl.BlockSpec(memory_space=pltpu.HBM)] * 8,
        out_specs=(vmem,) * 4,
        scratch_shapes=[
            pltpu.VMEM((ROWS, D), BF16),
            pltpu.VMEM((ROWS, H), BF16),
            pltpu.VMEM((1, 32), I32),
            pltpu.VMEM((8, 128), I32),
            pltpu.VMEM((8, 128), I32),
            pltpu.VMEM((SH, H), F32),
            pltpu.VMEM((SH, H), F32),
            pltpu.VMEM((SH, H), F32),
            pltpu.VMEM((SH, H), BF16),
            pltpu.VMEM((4, 2, SH, H), BF16),
            pltpu.VMEM((2, 2, ROWS, H), BF16),
            pltpu.VMEM((2, 8 * BL, H), BF16),
            pltpu.VMEM((CH, CH), BF16),
            pltpu.VMEM((4, 2, SH // 2, H), BF16),
            pltpu.VMEM((2, 4, 2, SH // 2, H), BF16),
            pltpu.VMEM((2, 4, SH // 2, H), BF16),
            pltpu.VMEM((2, 4, 2, SH // 2, H), BF16),
            pltpu.VMEM((2, SH // 2, H), BF16),
            pltpu.VMEM((2, 2, SH // 2, H), BF16),
            pltpu.VMEM((2, SH // 2, H), BF16),
            pltpu.VMEM((2, 2, SH // 2, H), BF16),
            pltpu.VMEM((4, SH, H), F32),
            pltpu.SemaphoreType.DMA((N_SEM,)),
            pltpu.SemaphoreType.DMA((N_SEM,)),
            pltpu.SemaphoreType.DMA((8,)),
            *[pltpu.VMEM((2, 4 * BL, n), BF16) for n in WIDTHS],
            *[pltpu.VMEM((4 * BL, n), BF16) for n in WIDTHS],
            *[pltpu.VMEM((4, BL, n), BF16) for n in WIDTHS],
            *[pltpu.VMEM((8, 32, n), BF16) for n in WIDTHS],
            *[pltpu.VMEM((2, 2, 2, 32, n), BF16) for n in WIDTHS],
        ],
        compiler_params=pltpu.CompilerParams(
            collective_id=0, has_side_effects=True, vmem_limit_bytes=56 * 2**20
        ),
    )(
        expert_inputs, hidden_grads, row_counts.reshape(1, 32), top_ids.T, route_slots.T,
        master[0], first[0], second[0],
    )
    return out, new_master[None], new_first[None], new_second[None]


def solution(mesh):
    rows = P(("dp", "ep"), None)
    weights = P("ep", "dp", None)
    return jax.shard_map(
        body,
        mesh=mesh,
        in_specs=(rows, rows, P(("dp", "ep")), rows, rows, weights, weights, weights),
        out_specs=(rows, weights, weights, weights),
        check_vma=False,
    )
```

time: 80.1 us -> 67.2 us (0.84)
  Pallas kernels: 68.7 us -> 61.1 us
  local copies, waits for them, and re-layouts: 10.4 us -> 5.24 us
    pallas_call x1, Pallas kernels: 68.7 us -> 61.1 us  [body(): pl.pallas_call(kernel, out_shape=(jax.ShapeDtypeStruct((128, D), BF16), s...]
    unnamed x20 -> x8, local copies, waits for them, and re-layouts: 10.4 us -> 5.24 us
where the time goes in v2:
time: 67.2 us; the launch traced here: 67 us
  Pallas kernels  61.1 us (91%)
  local copies, waits for them, and re-layouts  5.24 us (8%)
    pallas_call x1, Pallas kernels, body(): pl.pallas_call(kernel, out_shape=(jax.ShapeDtypeStruct((128, D), BF16), s...  61.1 us
    unnamed x8, local copies, waits for them, and re-layouts  5.24 us

profile of v2, /device:TPU:1, one launch (start us, length us, event | category | flops | bytes accessed | tf_op | source)
XLA Modules:
  0.0 67.0 jit_solution(11773543898816508103)
XLA Ops:
  0.6 61.1 %shard_map.111 = (bf16[128,3584]{1,0:T(8,128)(2,1)}, f32[224,256]{1,0:T(8,128)}, f32[224,256]{1,0:T(8,128)}, f32[224,256]{1,0:T(8,128)}) custom-call(bf16[320,3584]{1,0:T(8,128)(2,1)} %x_hbm.1, bf16[320,256]{1,0:T(8,128)(2,1)} %hg_hbm.1, s32[1,32]{1,0:T(1,128)} %bitcast.17, s32[8,128]{1,0:T(8,128)} %bitcast.15, s32[8,128]{1,0:T(8,128)} %bitcast.16, ...), custom_call_target="tpu_custom_call" | custom-call | tf_op jit(solution)/shard_map/pallas_call | solution.py:415
  61.7 0.0 copy-start.1
  61.7 0.0 copy-start
  61.8 2.2 %copy.16 = bf16[128,3584]{1,0:T(8,128)(2,1)} copy(bf16[128,3584]{1,0:T(8,128)(2,1)} %get-tuple-element.16) | data formatting | bytes 1835008
  64.0 1.6 %copy.17 = f32[1,224,256]{2,1,0:T(8,128)} copy(f32[1,224,256]{2,1,0:T(8,128)} %bitcast.11) | data formatting | bytes 458752
  65.6 0.0 copy-done.1
  65.6 0.7 %copy.18 = f32[1,224,256]{2,1,0:T(8,128)} copy(f32[1,224,256]{2,1,0:T(8,128)S(1)} %bitcast.10) | data formatting | bytes 458752
  66.3 0.0 copy-done
  66.3 0.7 %copy.19 = f32[1,224,256]{2,1,0:T(8,128)} copy(f32[1,224,256]{2,1,0:T(8,128)S(1)} %bitcast.9) | data formatting | bytes 458752
Async XLA Ops:
  61.7 3.9 %copy-start.1 = (f32[224,256]{1,0:T(8,128)S(1)}, f32[224,256]{1,0:T(8,128)}, u32[]{:S(2)}) copy-start(f32[224,256]{1,0:T(8,128)} %get-tuple-element.10) | copy-start | bytes 688132
  61.7 4.6 %copy-start = (f32[224,256]{1,0:T(8,128)S(1)}, f32[224,256]{1,0:T(8,128)}, u32[]{:S(2)}) copy-start(f32[224,256]{1,0:T(8,128)} %get-tuple-element.11) | copy-start | bytes 688132

commit v3 on v2

--- a/solution.py
+++ b/solution.py
@@ -20,32 +20,35 @@
 D = 3584
 H = 256
 SH = 224
+PART = 112
 CH = 896
 CAP = 10
 ROWS = 320
 BL = 80
 N_SEM = 128
-UNITS = (((0, 0, 224), (1, 0, 208), (3, 0, 208)), ((1, 208, 16), (3, 208, 16), (2, 0, 224)))
-WIDTHS = tuple(sum(n for _, _, n in unit) for unit in UNITS)
-PLACES = (0, WIDTHS[0])
+UNITS = (((0, 0, 112), (1, 0, 112), (3, 0, 32)), ((3, 32, 80), (2, 0, 112)))
+FILL = (0, 64)
+WIDTHS = tuple(sum(n for _, _, n in unit) + fill for unit, fill in zip(UNITS, FILL))
+PLACES = tuple(sum(WIDTHS[:u]) for u in range(len(WIDTHS)))
 
 
 def kernel(
     x_hbm, hg_hbm, cnt_hbm, ids_hbm, slots_hbm, mw_hbm, m1_hbm, m2_hbm,
+    out_hbm, nw_hbm, n1_hbm, n2_hbm,
     out_ref, nw_ref, n1_ref, n2_ref,
     x_ref, hg_ref, cnt_ref, ids_ref, slots_ref, mw_ref, m1_ref, m2_ref,
-    wown, wbuf, hgall, hgp, place, sopp, sside, rx1, rx2, ysopp, ysside, ry1, ry2, gown,
+    wown, wz, wbuf, hgall, hgp, place, sopp, sside, rx1, rx2, ysopp, ysside, ry1, ry2, gown,
     ssem, rsem, lsem, *by_unit,
 ):
     n_units = len(UNITS)
-    res, rcv1, rcv2, outg, fin = (by_unit[n_units * n : n_units * (n + 1)] for n in range(5))
+    res, rcv, outg, fin = (by_unit[n_units * n : n_units * (n + 1)] for n in range(4))
 
     dp = lax.axis_index("dp")
     ep = lax.axis_index("ep")
     x, y = dp // 4, dp % 4
     yl, z, c = ep // 16, (ep // 2) % 8, ep % 2
-    odd = z % 2
-    sgn = 2 * odd - 1
+    b = z % 2
+    zq = z + 1 - 2 * b
     sib = 1 - c
     xs = ((x + 1) % 4, (x + 3) % 4)
     ys = ((y + 1) % 4, (y + 3) % 4)
@@ -88,7 +91,7 @@
     barrier = pltpu.get_barrier_semaphore()
     near = [dev(cc=sib), dev(xx=xs[0]), dev(xx=xs[1])]
     near += [dev(yy=yy, cc=cc) for yy in ys for cc in (c, sib)]
-    near += [dev(zz=(z + t) % 8) for t in (1, 2, 3, 5, 6, 7)]
+    near += [dev(zz=(z + t) % 8) for t in range(1, 8)]
     near += [dev(xx=xp, cc=sib), dev(xx=xw, cc=sib)]
     near += [dev(xx=xx, ll=1 - yl, cc=cc) for xx in (x, xp) for cc in (c, sib)]
     for to in near:
@@ -104,13 +107,13 @@
         loads[name].start()
 
     loads["mw"].wait()
-    wown[...] = mw_ref[...].astype(BF16)
+    wown[...] = mw_ref[...].astype(BF16).reshape(2, PART, H)
     is_a = c == 0
     not_a = c == 1
 
     @pl.when(is_a)
     def _():
-        wbuf[y, c] = wown[...]
+        wbuf[y, 0, c] = wown[b]
 
     def dw_chunk(at):
         cols = pl.ds(pl.multiple_of(at * CH, 128), CH)
@@ -118,20 +121,27 @@
 
     pl.semaphore_wait(barrier, len(near))
 
-    s_wy = [sem("wy_up", 2), sem("wy_down", 2)]
-    s_wsib = sem("wsib")
-    for k in (0, 1):
-        send(wown, wbuf.at[y, c], s_wy[k] + c, dev(yy=ys[k], cc=0))
-
-    @pl.when(not_a)
-    def _():
-        send(wown, wbuf.at[y, c], s_wsib, dev(cc=sib))
+    s_wz = sem("wz")
+    s_wy = [sem("wy_up", 4), sem("wy_down", 4)]
+    s_wsib = sem("wsib", 2)
+    send(wown.at[1 - b], wz, s_wz, dev(zz=zq))
+
+    def to_y(rel, here):
+        for k in (0, 1):
+            send(here, wbuf.at[y, rel, c], s_wy[k] + 2 * rel + c, dev(yy=ys[k], cc=0))
+
+        @pl.when(not_a)
+        def _():
+            send(here, wbuf.at[y, rel, c], s_wsib + rel, dev(cc=sib))
+
+    to_y(0, wown.at[b])
 
     loads["hg"].wait()
-    s_hg = sem("hg", 3)
-    hgall[0, c] = hg_ref[...]
-    send(hgall.at[0, c], hgall.at[1, c], s_hg, dev(xx=xp))
-    send(hgall.at[0, c], hgall.at[0, c], s_hg + 1, dev(cc=sib))
+    s_hg = sem("hg", 7)
+    hgall[0, 0, c] = hg_ref[...]
+    send(hgall.at[0, 0, c], hgall.at[1, 0, c], s_hg + 2, dev(xx=xp))
+    send(hgall.at[0, 0, c], hgall.at[0, 1, c], s_hg + 1, dev(zz=zq))
+    send(hgall.at[0, 0, c], hgall.at[0, 0, c], s_hg, dev(cc=sib))
     loads["cnt"].wait()
 
     row = lax.broadcasted_iota(I32, (ROWS, 32), 0)
@@ -149,7 +159,7 @@
     u3 = v3 - 20 * l3
     c3 = jnp.where(u3 >= 10, 1, 0)
     p3 = u3 - 10 * c3
-    z3 = (jnp.where(b3 < 4, z + sgn * b3, z - sgn * (b3 - 3)) + 16) & 7
+    z3 = (z + b3) & 7
     source = (r3 * ROWS + (l3 * 16 + z3 * 2 + c3) * CAP + p3).reshape(8 * BL, 1)
     perm = jnp.where(lax.broadcasted_iota(I32, (8 * BL, 2 * ROWS), 1) == source, 1.0, 0.0).astype(BF16)
 
@@ -175,23 +185,35 @@
         sside[k] = dw_chunk(xs[k]).astype(BF16).reshape(4, 2, part, H)
     gown[...] = dw_chunk(x).reshape(4, SH, H)
 
+    arrived(wz, s_wz)
+    to_y(1, wz)
+
+    @pl.when(is_a)
+    def _():
+        wbuf[y, 1, c] = wz[...]
+
     s_wyf = [sem("wyf_up"), sem("wyf_down")]
     s_wx = sem("wx", 4)
     order = (0, 3, 1, 2)
 
     def half_of(d, k):
-        return wbuf.at[yat(d), :, pl.ds(k * part, part)]
+        return wbuf.at[yat(d), k]
 
     def spread(d):
         send(wbuf.at[yat(d)], wbuf.at[yat(d)], s_wx + d, dev(xx=xw, cc=sib))
 
+    def gather_a_first():
+        for rel in (0, 1):
+            arrived(wbuf.at[y, rel, sib], s_wsib + rel)
+        spread(0)
+
     def gather_a():
-        arrived(wbuf.at[y, sib], s_wsib)
-        spread(0)
         for k, d in ((0, 3), (1, 1)):
-            for s in (0, 1):
-                arrived(wbuf.at[yat(d), s], s_wy[k] + s)
-            send(half_of(d, k), half_of(d, k), s_wyf[k], dev(yy=ys[k]))
+            for rel in (0, 1):
+                for cc in (0, 1):
+                    arrived(wbuf.at[yat(d), rel, cc], s_wy[k] + 2 * rel + cc)
+                if rel == k:
+                    send(half_of(d, k), half_of(d, k), s_wyf[k], dev(yy=ys[k]))
             spread(d)
 
     def gather_a_last():
@@ -206,34 +228,42 @@
     def gather_b_last():
         arrived(wbuf.at[y2], s_wx + 2)
 
+    def pass_on():
+        arrived(hgall.at[1, 0, c], s_hg + 2)
+        send(hgall.at[1, 0, c], hgall.at[1, 1, c], s_hg + 4, dev(zz=zq))
+        send(hgall.at[1, 0, c], hgall.at[1, 0, c], s_hg + 3, dev(cc=sib))
+        arrived(hgall.at[0, 1, c], s_hg + 1)
+        send(hgall.at[0, 1, c], hgall.at[0, 1, c], s_hg + 5, dev(cc=sib))
+
     def rows_in():
-        arrived(hgall.at[1, c], s_hg)
-        send(hgall.at[1, c], hgall.at[1, c], s_hg + 2, dev(cc=sib))
-        arrived(hgall.at[0, sib], s_hg + 1)
-        arrived(hgall.at[1, sib], s_hg + 2)
-        for s in (0, 1):
-            both = jnp.concatenate([hgall[0, s], hgall[1, s]], axis=0)
-            hgp[s] = jnp.dot(perm, both, preferred_element_type=F32).astype(BF16)
-
-    n_units = len(UNITS)
-    s_r1 = sem("rows1", n_units)
-    s_r2 = sem("rows2", 4 * n_units)
+        arrived(hgall.at[1, 1, c], s_hg + 4)
+        send(hgall.at[1, 1, c], hgall.at[1, 1, c], s_hg + 6, dev(cc=sib))
+        arrived(hgall.at[0, 0, sib], s_hg)
+        arrived(hgall.at[1, 0, sib], s_hg + 3)
+        arrived(hgall.at[0, 1, sib], s_hg + 5)
+        arrived(hgall.at[1, 1, sib], s_hg + 6)
+        for rel in (0, 1):
+            for cc in (0, 1):
+                both = jnp.concatenate([hgall[0, rel, cc], hgall[1, rel, cc]], axis=0)
+                hgp[rel, cc] = jnp.dot(perm, both, preferred_element_type=F32).astype(BF16)
+
+    s_rows = sem("rows", 8 * n_units)
     s_fin = sem("fin", 8 * n_units)
+    far = (4, 3, 5, 2, 6, 1, 7)
 
     def rows_one(u):
         total = jnp.zeros((8 * BL, WIDTHS[u]), F32)
-        for s in (0, 1):
-            weights = jnp.concatenate([wbuf[yat(d), s, pl.ds(at, n)] for d, at, n in UNITS[u]], axis=0)
-            total += lax.dot_general(hgp[s], weights, (((1,), (1,)), ((), ())), preferred_element_type=F32)
-        res[u][...] = total.astype(BF16).reshape(2, 4 * BL, WIDTHS[u])
-        send(res[u].at[1], rcv1[u], s_r1 + u, dev(zz=(z - sgn + 8) % 8))
-
-    def rows_two(u):
-        arrived(rcv1[u], s_r1 + u)
-        res[u][0] = (res[u][0].astype(F32) + rcv1[u][...].astype(F32)).astype(BF16)
-        for t in (3, 2, 1):
-            send(res[u].at[0, pl.ds(t * BL, BL)], rcv2[u].at[t], s_r2 + 4 * u + t, dev(zz=(z + sgn * t + 8) % 8))
-        rcv2[u][0] = res[u][0, pl.ds(0, BL)]
+        for rel in (0, 1):
+            for cc in (0, 1):
+                pieces = [wbuf[yat(d), rel, cc, pl.ds(at, n)] for d, at, n in UNITS[u]]
+                if FILL[u]:
+                    pieces.append(wbuf[y, rel, cc, pl.ds(0, FILL[u])])
+                weights = jnp.concatenate(pieces, axis=0)
+                total += lax.dot_general(hgp[rel, cc], weights, (((1,), (1,)), ((), ())), preferred_element_type=F32)
+        res[u][...] = total.astype(BF16).reshape(8, BL, WIDTHS[u])
+        for i in far:
+            send(res[u].at[i], rcv[u].at[i % 2, i // 2], s_rows + 8 * u + i, dev(zz=(z + i) % 8))
+        rcv[u][0, 0] = res[u][0]
 
     rr = lax.broadcasted_iota(I32, (256, 4 * BL), 0)
     col = lax.broadcasted_iota(I32, (1, 4 * BL), 1)
@@ -244,19 +274,22 @@
     gg = jnp.zeros_like(col)
     for g in range(1, 8):
         gg = gg + jnp.where(ww >= g * CAP, 1, 0)
-    expert = jnp.zeros_like(col)
-    for t in range(4):
-        step = -sgn * t if t % 2 == 0 else sgn * t
-        expert = jnp.where(tt == t, ((z + step + 8) % 8) // 4, expert)
-    target = gg * 32 + expert * CAP + ww - CAP * gg
-    sorting = jnp.where(rr == target, 1.0, 0.0).astype(BF16)
+
+    def sorting(par):
+        expert = jnp.where(((z + 16 - 2 * tt - par) & 7) >= 4, 1, 0)
+        target = gg * 32 + expert * CAP + ww - CAP * gg
+        return jnp.where(rr == target, 1.0, 0.0).astype(BF16)
+
     owners = [(rep, ll, cc) for rep in (1, 0) for ll in (1 - yl, yl) for cc in (c, sib)]
 
-    def rows_three(u):
-        for t in (1, 2, 3):
-            arrived(rcv2[u].at[t], s_r2 + 4 * u + t)
-        rows = jnp.dot(sorting, rcv2[u][...].reshape(4 * BL, WIDTHS[u]), preferred_element_type=F32)
-        outg[u][...] = rows.astype(BF16).reshape(8, 32, WIDTHS[u])
+    def rows_two(u):
+        for par in (0, 1):
+            for t in range(4):
+                i = 2 * t + par
+                if i:
+                    arrived(rcv[u].at[par, t], s_rows + 8 * u + i)
+            rows = jnp.dot(sorting(par), rcv[u][par].reshape(4 * BL, WIDTHS[u]), preferred_element_type=F32)
+            outg[u][:, par] = rows.astype(BF16).reshape(8, 32, WIDTHS[u])
         for k, (rep, ll, cc) in enumerate(owners):
             if k == 6:
                 fin[u][0, c, yl] = outg[u][yl * 2 + c]
@@ -290,6 +323,8 @@
             ysside[k, k] = (rows[k] + ry1[k].astype(F32)).astype(BF16)
             ysside[k, 1 - k] = rows[1 - k].astype(BF16)
             send(ysside.at[k], ry2.at[k], s_ry2[k], dev(yy=ys[k]))
+
+    leaves = []
 
     def adam():
         grads = over_x(0)
@@ -308,43 +343,51 @@
         )
         n1_ref[...] = new_first
         n2_ref[...] = new_second
-
-    from_col = lax.broadcasted_iota(I32, (CH, 1), 0)
+        for n, (here, there) in enumerate(((nw_ref, nw_hbm), (n1_ref, n1_hbm), (n2_ref, n2_hbm))):
+            leaves.append(pltpu.make_async_copy(here, there, lsem.at[8 + n]))
+            leaves[-1].start()
+
+    from_col = lax.broadcasted_iota(I32, (PLACES[-1] + WIDTHS[-1], 1), 0)
     belongs = jnp.zeros_like(from_col)
-    done = 0
-    for unit in UNITS:
-        for d, at, n in unit:
+    for u in range(n_units):
+        done = PLACES[u]
+        for d, at, n in UNITS[u]:
             belongs = jnp.where(from_col >= done, yat(d) * SH + at + from_col - done, belongs)
             done += n
-    place[...] = jnp.where(lax.broadcasted_iota(I32, (CH, CH), 1) == belongs, 1.0, 0.0).astype(BF16)
+        if FILL[u]:
+            belongs = jnp.where(from_col >= done, -SH, belongs)
+    to_col = lax.broadcasted_iota(I32, (PLACES[-1] + WIDTHS[-1], CH), 1)
+    for par in (0, 1):
+        rows_of = b if par == 0 else 1 - b
+        place[par] = jnp.where(to_col == belongs + rows_of * PART, 1.0, 0.0).astype(BF16)
 
     @pl.when(is_a)
     def _():
+        gather_a_first()
+        grads_one()
+        pass_on()
         gather_a()
-        grads_one()
         rows_in()
         rows_one(0)
         gather_a_last()
         rows_one(1)
         grads_two()
-        rows_two(0)
 
     @pl.when(not_a)
     def _():
         grads_one()
+        pass_on()
         rows_in()
         gather_b()
         rows_one(0)
         grads_two()
         gather_b_last()
         rows_one(1)
-        rows_two(0)
-
+
+    grads_three()
+    rows_two(0)
+    grads_four()
     rows_two(1)
-    grads_three()
-    rows_three(0)
-    grads_four()
-    rows_three(1)
     adam()
 
     wanted = lax.broadcasted_iota(I32, (64, 128), 0)
@@ -370,32 +413,38 @@
         for cc in (0, 1):
             natural = jnp.zeros((64, CH), F32)
             for u in range(n_units):
-                natural += jnp.dot(
-                    fin[u][rep, cc].reshape(64, WIDTHS[u]), place[pl.ds(PLACES[u], WIDTHS[u])],
-                    preferred_element_type=F32,
-                )
+                for par in (0, 1):
+                    natural += jnp.dot(
+                        fin[u][rep, cc, :, par].reshape(64, WIDTHS[u]), place[par, pl.ds(PLACES[u], WIDTHS[u])],
+                        preferred_element_type=F32,
+                    )
             from_x = (x, xp)[rep]
             chunk = (from_x, 3 - from_x)[cc]
-            out_ref[:, pl.ds(pl.multiple_of(chunk * CH, 128), CH)] = lax.dot_general(
+            out_ref[rep, cc] = lax.dot_general(
                 table, natural.astype(BF16), (((0,), (0,)), ((), ())), preferred_element_type=F32
             ).astype(BF16)
-
+            there = out_hbm.at[:, pl.ds(pl.multiple_of(chunk * CH, 128), CH)]
+            leaves.append(pltpu.make_async_copy(out_ref.at[rep, cc], there, lsem.at[11 + 2 * rep + cc]))
+            leaves[-1].start()
+
+    for leaf in leaves:
+        leaf.wait()
     for k in (0, 1):
-        sent(wown, s_wy[k] + c)
+        for rel in (0, 1):
+            sent(wz, s_wy[k] + 2 * rel + c)
         for d in order:
             sent(sopp.at[yat(d), k], s_rx1[k] + d)
             sent(sside.at[k, yat(d)], s_rx2[k] + d)
         sent(ysopp.at[k], s_ry1[k])
         sent(ysside.at[k], s_ry2[k])
+    sent(wz, s_wz)
     for u in range(n_units):
-        sent(res[u].at[1], s_r1 + u)
-        for t in (1, 2, 3):
-            sent(res[u].at[0, pl.ds(t * BL, BL)], s_r2 + 4 * u + t)
+        for i in far:
+            sent(res[u].at[i], s_rows + 8 * u + i)
         for k in (0, 1, 2, 3, 4, 5, 7):
             sent(outg[u].at[k], s_fin + 8 * u + k)
-    for k in (0, 1):
-        sent(hgall.at[0, c], s_hg + k)
-    sent(hgall.at[1, c], s_hg + 2)
+    for k in range(7):
+        sent(hgall.at[0, 0, c], s_hg + k)
 
     @pl.when(is_a)
     def _():
@@ -406,18 +455,36 @@
 
     @pl.when(not_a)
     def _():
-        sent(wown, s_wsib)
+        for rel in (0, 1):
+            sent(wz, s_wsib + rel)
+
+
+def hand_over(*refs):
+    there, held, back, sems = refs[:4], refs[8:12], refs[4:8], refs[12]
+    loads = [pltpu.make_async_copy(there[n], held[n], sems.at[n]) for n in range(4)]
+    stores = [pltpu.make_async_copy(held[n], back[n], sems.at[4 + n]) for n in range(4)]
+    for load in loads:
+        load.start()
+    for load, store in zip(loads, stores):
+        load.wait()
+        store.start()
+    for store in stores:
+        store.wait()
 
 
 def body(expert_inputs, hidden_grads, row_counts, top_ids, route_slots, master, first, second):
-    vmem = pl.BlockSpec(memory_space=pltpu.VMEM)
+    hbm = pl.BlockSpec(memory_space=pltpu.HBM)
     shard = jax.ShapeDtypeStruct((SH, H), F32)
-    out, new_master, new_first, new_second = pl.pallas_call(
+    results = pl.pallas_call(
         kernel,
         out_shape=(jax.ShapeDtypeStruct((128, D), BF16), shard, shard, shard),
-        in_specs=[pl.BlockSpec(memory_space=pltpu.HBM)] * 8,
-        out_specs=(vmem,) * 4,
+        in_specs=[hbm] * 8,
+        out_specs=(hbm,) * 4,
         scratch_shapes=[
+            pltpu.VMEM((2, 2, 128, CH), BF16),
+            pltpu.VMEM((SH, H), F32),
+            pltpu.VMEM((SH, H), F32),
+            pltpu.VMEM((SH, H), F32),
             pltpu.VMEM((ROWS, D), BF16),
             pltpu.VMEM((ROWS, H), BF16),
             pltpu.VMEM((1, 32), I32),
@@ -426,11 +493,12 @@
             pltpu.VMEM((SH, H), F32),
             pltpu.VMEM((SH, H), F32),
             pltpu.VMEM((SH, H), F32),
-            pltpu.VMEM((SH, H), BF16),
-            pltpu.VMEM((4, 2, SH, H), BF16),
-            pltpu.VMEM((2, 2, ROWS, H), BF16),
-            pltpu.VMEM((2, 8 * BL, H), BF16),
-            pltpu.VMEM((CH, CH), BF16),
+            pltpu.VMEM((2, PART, H), BF16),
+            pltpu.VMEM((PART, H), BF16),
+            pltpu.VMEM((4, 2, 2, PART, H), BF16),
+            pltpu.VMEM((2, 2, 2, ROWS, H), BF16),
+            pltpu.VMEM((2, 2, 8 * BL, H), BF16),
+            pltpu.VMEM((2, PLACES[-1] + WIDTHS[-1], CH), BF16),
             pltpu.VMEM((4, 2, SH // 2, H), BF16),
             pltpu.VMEM((2, 4, 2, SH // 2, H), BF16),
             pltpu.VMEM((2, 4, SH // 2, H), BF16),
@@ -442,12 +510,11 @@
             pltpu.VMEM((4, SH, H), F32),
             pltpu.SemaphoreType.DMA((N_SEM,)),
             pltpu.SemaphoreType.DMA((N_SEM,)),
-            pltpu.SemaphoreType.DMA((8,)),
-            *[pltpu.VMEM((2, 4 * BL, n), BF16) for n in WIDTHS],
-            *[pltpu.VMEM((4 * BL, n), BF16) for n in WIDTHS],
-            *[pltpu.VMEM((4, BL, n), BF16) for n in WIDTHS],
-            *[pltpu.VMEM((8, 32, n), BF16) for n in WIDTHS],
-            *[pltpu.VMEM((2, 2, 2, 32, n), BF16) for n in WIDTHS],
+            pltpu.SemaphoreType.DMA((16,)),
+            *[pltpu.VMEM((8, BL, n), BF16) for n in WIDTHS],
+            *[pltpu.VMEM((2, 4, BL, n), BF16) for n in WIDTHS],
+            *[pltpu.VMEM((8, 2, 32, n), BF16) for n in WIDTHS],
+            *[pltpu.VMEM((2, 2, 2, 2, 32, n), BF16) for n in WIDTHS],
         ],
         compiler_params=pltpu.CompilerParams(
             collective_id=0, has_side_effects=True, vmem_limit_bytes=56 * 2**20
@@ -456,6 +523,18 @@
         expert_inputs, hidden_grads, row_counts.reshape(1, 32), top_ids.T, route_slots.T,
         master[0], first[0], second[0],
     )
+    out, new_master, new_first, new_second = pl.pallas_call(
+        hand_over,
+        out_shape=(jax.ShapeDtypeStruct((128, D), BF16), shard, shard, shard),
+        in_specs=[hbm] * 4,
+        out_specs=(hbm,) * 4,
+        scratch_shapes=[
+            pltpu.VMEM((128, D), BF16),
+            *[pltpu.VMEM((SH, H), F32)] * 3,
+            pltpu.SemaphoreType.DMA((8,)),
+        ],
+        compiler_params=pltpu.CompilerParams(vmem_limit_bytes=56 * 2**20),
+    )(*results)
     return out, new_master[None], new_first[None], new_second[None]
 
 

time: 67.2 us -> 59.7 us (0.89)
  local copies, waits for them, and re-layouts: 5.24 us -> 0 us
  Pallas kernels: 61.1 us -> 58.8 us
    unnamed x8 -> x0, local copies, waits for them, and re-layouts: 5.24 us -> none
    pallas_call x1, Pallas kernels: 61.1 us -> 56.4 us  [body(): pl.pallas_call(kernel, out_shape=(jax.ShapeDtypeStruct((128, D), BF16), s...]
    pallas_call x0 -> x1, Pallas kernels: none -> 2.39 us  [body(): pl.pallas_call(hand_over, out_shape=(jax.ShapeDtypeStruct((128, D), BF16)...]
where the time goes in v3:
time: 59.7 us; the launch traced here: 59.4 us
  Pallas kernels  58.8 us (98%)
  between operations  0.64 us (1%)
    pallas_call x1, Pallas kernels, body(): pl.pallas_call(kernel, out_shape=(jax.ShapeDtypeStruct((128, D), BF16), s...  56.4 us
    pallas_call x1, Pallas kernels, body(): pl.pallas_call(hand_over, out_shape=(jax.ShapeDtypeStruct((128, D), BF16)...  2.39 us

profile of v3, /device:TPU:1, one launch (start us, length us, event | category | flops | bytes accessed | tf_op | source)
XLA Modules:
  0.0 59.4 jit_solution(10431643382101713195)
XLA Ops:
  0.6 56.4 %shard_map.111 = (bf16[128,3584]{1,0:T(8,128)(2,1)}, f32[224,256]{1,0:T(8,128)}, f32[224,256]{1,0:T(8,128)}, f32[224,256]{1,0:T(8,128)}) custom-call(bf16[320,3584]{1,0:T(8,128)(2,1)} %x_hbm.1, bf16[320,256]{1,0:T(8,128)(2,1)} %hg_hbm.1, s32[1,32]{1,0:T(1,128)} %bitcast.14, s32[8,128]{1,0:T(8,128)} %bitcast.12, s32[8,128]{1,0:T(8,128)} %bitcast.13, ...), custom_call_target="tpu_custom_call" | custom-call | tf_op jit(solution)/shard_map/pallas_call | solution.py:478
  57.0 2.4 %shard_map.112 = (bf16[128,3584]{1,0:T(8,128)(2,1)}, f32[224,256]{1,0:T(8,128)}, f32[224,256]{1,0:T(8,128)}, f32[224,256]{1,0:T(8,128)}) custom-call(bf16[128,3584]{1,0:T(8,128)(2,1)} %get-tuple-element.12.refs_0_, f32[224,256]{1,0:T(8,128)} %get-tuple-element.13.refs_1_, f32[224,256]{1,0:T(8,128)} %get-tuple-element.14.refs_2_, ...), custom_call_target="tpu_custom_call" | custom-call | tf_op jit(solution)/shard_map/pallas_call | solution.py:526

commit v4 on v3

--- a/solution.py
+++ b/solution.py
@@ -27,8 +27,7 @@
 BL = 80
 N_SEM = 128
 UNITS = (((0, 0, 112), (1, 0, 112), (3, 0, 32)), ((3, 32, 80), (2, 0, 112)))
-FILL = (0, 64)
-WIDTHS = tuple(sum(n for _, _, n in unit) + fill for unit, fill in zip(UNITS, FILL))
+WIDTHS = tuple(sum(n for _, _, n in unit) for unit in UNITS)
 PLACES = tuple(sum(WIDTHS[:u]) for u in range(len(WIDTHS)))
 
 
@@ -151,6 +150,24 @@
     alive = jnp.sum(jnp.where(alive, 1.0, 0.0), axis=1, keepdims=True) > 0.5
     masked = jnp.where(alive, hg_ref[...].astype(F32), 0.0).astype(BF16)
 
+    loads["x"].wait()
+    part = SH // 2
+    s_rx1 = [sem("rx1_right", 4), sem("rx1_left", 4)]
+    s_rx2 = [sem("rx2_right", 4), sem("rx2_left", 4)]
+    s_ry1 = [sem("ry1_up"), sem("ry1_down")]
+    s_ry2 = [sem("ry2_up"), sem("ry2_down")]
+    far_first = (2, 1, 3, 0)
+
+    def yat(d):
+        return (y + d) % 4
+
+    sopp[...] = dw_chunk(x2).astype(BF16).reshape(4, 2, part, H)
+
+    def grads_one(k):
+        for d in far_first:
+            send(sopp.at[yat(d), k], rx1.at[k, yat(d)], s_rx1[0] + 4 * k + d, dev(xx=(x + 1 + 2 * k) % 4))
+
+    grads_one(1 - x % 2)
     b3 = lax.broadcasted_iota(I32, (8, BL, 1), 0)
     w3 = lax.broadcasted_iota(I32, (8, BL, 1), 1)
     r3 = jnp.where(w3 >= 40, 1, 0)
@@ -163,24 +180,6 @@
     source = (r3 * ROWS + (l3 * 16 + z3 * 2 + c3) * CAP + p3).reshape(8 * BL, 1)
     perm = jnp.where(lax.broadcasted_iota(I32, (8 * BL, 2 * ROWS), 1) == source, 1.0, 0.0).astype(BF16)
 
-    loads["x"].wait()
-    part = SH // 2
-    s_rx1 = [sem("rx1_right", 4), sem("rx1_left", 4)]
-    s_rx2 = [sem("rx2_right", 4), sem("rx2_left", 4)]
-    s_ry1 = [sem("ry1_up"), sem("ry1_down")]
-    s_ry2 = [sem("ry2_up"), sem("ry2_down")]
-    far_first = (2, 1, 3, 0)
-
-    def yat(d):
-        return (y + d) % 4
-
-    sopp[...] = dw_chunk(x2).astype(BF16).reshape(4, 2, part, H)
-
-    def grads_one():
-        for d in far_first:
-            for k in (0, 1):
-                send(sopp.at[yat(d), k], rx1.at[k, yat(d)], s_rx1[k] + d, dev(xx=xs[k]))
-
     for k in (0, 1):
         sside[k] = dw_chunk(xs[k]).astype(BF16).reshape(4, 2, part, H)
     gown[...] = dw_chunk(x).reshape(4, SH, H)
@@ -229,23 +228,29 @@
         arrived(wbuf.at[y2], s_wx + 2)
 
     def pass_on():
+        sent(hgall.at[0, 0, c], s_hg + 2)
+        grads_one(x % 2)
         arrived(hgall.at[1, 0, c], s_hg + 2)
         send(hgall.at[1, 0, c], hgall.at[1, 1, c], s_hg + 4, dev(zz=zq))
         send(hgall.at[1, 0, c], hgall.at[1, 0, c], s_hg + 3, dev(cc=sib))
         arrived(hgall.at[0, 1, c], s_hg + 1)
         send(hgall.at[0, 1, c], hgall.at[0, 1, c], s_hg + 5, dev(cc=sib))
 
+    def sort_rows(rel, cc):
+        both = jnp.concatenate([hgall[0, rel, cc], hgall[1, rel, cc]], axis=0)
+        hgp[rel, cc] = jnp.dot(perm, both, preferred_element_type=F32).astype(BF16)
+
     def rows_in():
+        arrived(hgall.at[0, 0, sib], s_hg)
+        arrived(hgall.at[1, 0, sib], s_hg + 3)
+        sort_rows(0, 0)
+        sort_rows(0, 1)
         arrived(hgall.at[1, 1, c], s_hg + 4)
         send(hgall.at[1, 1, c], hgall.at[1, 1, c], s_hg + 6, dev(cc=sib))
-        arrived(hgall.at[0, 0, sib], s_hg)
-        arrived(hgall.at[1, 0, sib], s_hg + 3)
         arrived(hgall.at[0, 1, sib], s_hg + 5)
+        sort_rows(1, c)
         arrived(hgall.at[1, 1, sib], s_hg + 6)
-        for rel in (0, 1):
-            for cc in (0, 1):
-                both = jnp.concatenate([hgall[0, rel, cc], hgall[1, rel, cc]], axis=0)
-                hgp[rel, cc] = jnp.dot(perm, both, preferred_element_type=F32).astype(BF16)
+        sort_rows(1, sib)
 
     s_rows = sem("rows", 8 * n_units)
     s_fin = sem("fin", 8 * n_units)
@@ -256,8 +261,6 @@
         for rel in (0, 1):
             for cc in (0, 1):
                 pieces = [wbuf[yat(d), rel, cc, pl.ds(at, n)] for d, at, n in UNITS[u]]
-                if FILL[u]:
-                    pieces.append(wbuf[y, rel, cc, pl.ds(0, FILL[u])])
                 weights = jnp.concatenate(pieces, axis=0)
                 total += lax.dot_general(hgp[rel, cc], weights, (((1,), (1,)), ((), ())), preferred_element_type=F32)
         res[u][...] = total.astype(BF16).reshape(8, BL, WIDTHS[u])
@@ -297,12 +300,17 @@
             send(outg[u].at[rep * 4 + ll * 2 + cc], fin[u].at[rep, c, yl], s_fin + 8 * u + k,
                  dev(xx=(x, xp)[rep], ll=ll, cc=cc), s_fin + 8 * u + 4 * rep + 2 * c + yl)
 
-    def grads_two():
-        for d in far_first:
+    def grads_two(*blocks):
+        for d in blocks:
             for k in (0, 1):
                 arrived(rx1.at[k, yat(d)], s_rx1[k] + d)
                 sside[k, yat(d), k] = (sside[k, yat(d), k].astype(F32) + rx1[k, yat(d)].astype(F32)).astype(BF16)
                 send(sside.at[k, yat(d)], rx2.at[k, yat(d)], s_rx2[k] + d, dev(xx=xs[k]))
+
+    def side_sent(*blocks):
+        for d in blocks:
+            for k in (0, 1):
+                sent(sside.at[k, yat(d)], s_rx2[k] + d)
 
     def over_x(d):
         rows = gown[yat(d)]
@@ -347,6 +355,31 @@
             leaves.append(pltpu.make_async_copy(here, there, lsem.at[8 + n]))
             leaves[-1].start()
 
+    @pl.when(is_a)
+    def _():
+        gather_a_first()
+        pass_on()
+        gather_a()
+        grads_two(2)
+        rows_in()
+        rows_one(0)
+        gather_a_last()
+        rows_one(1)
+        side_sent(2)
+        grads_two(1, 3)
+
+    @pl.when(not_a)
+    def _():
+        pass_on()
+        grads_two(2)
+        rows_in()
+        gather_b()
+        rows_one(0)
+        gather_b_last()
+        rows_one(1)
+        side_sent(2)
+        grads_two(1, 3)
+
     from_col = lax.broadcasted_iota(I32, (PLACES[-1] + WIDTHS[-1], 1), 0)
     belongs = jnp.zeros_like(from_col)
     for u in range(n_units):
@@ -354,37 +387,14 @@
         for d, at, n in UNITS[u]:
             belongs = jnp.where(from_col >= done, yat(d) * SH + at + from_col - done, belongs)
             done += n
-        if FILL[u]:
-            belongs = jnp.where(from_col >= done, -SH, belongs)
     to_col = lax.broadcasted_iota(I32, (PLACES[-1] + WIDTHS[-1], CH), 1)
     for par in (0, 1):
         rows_of = b if par == 0 else 1 - b
         place[par] = jnp.where(to_col == belongs + rows_of * PART, 1.0, 0.0).astype(BF16)
 
-    @pl.when(is_a)
-    def _():
-        gather_a_first()
-        grads_one()
-        pass_on()
-        gather_a()
-        rows_in()
-        rows_one(0)
-        gather_a_last()
-        rows_one(1)
-        grads_two()
-
-    @pl.when(not_a)
-    def _():
-        grads_one()
-        pass_on()
-        rows_in()
-        gather_b()
-        rows_one(0)
-        grads_two()
-        gather_b_last()
-        rows_one(1)
-
     grads_three()
+    side_sent(1, 3)
+    grads_two(0)
     rows_two(0)
     grads_four()
     rows_two(1)
@@ -434,7 +444,7 @@
             sent(wz, s_wy[k] + 2 * rel + c)
         for d in order:
             sent(sopp.at[yat(d), k], s_rx1[k] + d)
-            sent(sside.at[k, yat(d)], s_rx2[k] + d)
+        sent(sside.at[k, y], s_rx2[k])
         sent(ysopp.at[k], s_ry1[k])
         sent(ysside.at[k], s_ry2[k])
     sent(wz, s_wz)
@@ -443,7 +453,7 @@
             sent(res[u].at[i], s_rows + 8 * u + i)
         for k in (0, 1, 2, 3, 4, 5, 7):
             sent(outg[u].at[k], s_fin + 8 * u + k)
-    for k in range(7):
+    for k in (0, 1, 3, 4, 5, 6):
         sent(hgall.at[0, 0, c], s_hg + k)
 
     @pl.when(is_a)

time: 59.7 us -> 57.2 us (0.958)
  Pallas kernels: 58.8 us -> 56.4 us
    pallas_call x1, Pallas kernels: 56.4 us -> 54 us  [body(): pl.pallas_call(kernel, out_shape=(jax.ShapeDtypeStruct((128, D), BF16), s...]
where the time goes in v4:
time: 57.2 us; the launch traced here: 57 us
  Pallas kernels  56.4 us (99%)
  between operations  0.64 us (1%)
    pallas_call x1, Pallas kernels, body(): pl.pallas_call(kernel, out_shape=(jax.ShapeDtypeStruct((128, D), BF16), s...  54 us
    pallas_call x1, Pallas kernels, body(): pl.pallas_call(hand_over, out_shape=(jax.ShapeDtypeStruct((128, D), BF16)...  2.39 us

profile of v4, /device:TPU:1, one launch (start us, length us, event | category | flops | bytes accessed | tf_op | source)
XLA Modules:
  0.0 57.0 jit_solution(423398958978835505)
XLA Ops:
  0.6 54.0 %shard_map.111 = (bf16[128,3584]{1,0:T(8,128)(2,1)}, f32[224,256]{1,0:T(8,128)}, f32[224,256]{1,0:T(8,128)}, f32[224,256]{1,0:T(8,128)}) custom-call(bf16[320,3584]{1,0:T(8,128)(2,1)} %x_hbm.1, bf16[320,256]{1,0:T(8,128)(2,1)} %hg_hbm.1, s32[1,32]{1,0:T(1,128)} %bitcast.14, s32[8,128]{1,0:T(8,128)} %bitcast.12, s32[8,128]{1,0:T(8,128)} %bitcast.13, ...), custom_call_target="tpu_custom_call" | custom-call | tf_op jit(solution)/shard_map/pallas_call | solution.py:488
  54.6 2.4 %shard_map.112 = (bf16[128,3584]{1,0:T(8,128)(2,1)}, f32[224,256]{1,0:T(8,128)}, f32[224,256]{1,0:T(8,128)}, f32[224,256]{1,0:T(8,128)}) custom-call(bf16[128,3584]{1,0:T(8,128)(2,1)} %get-tuple-element.12.refs_0_, f32[224,256]{1,0:T(8,128)} %get-tuple-element.13.refs_1_, f32[224,256]{1,0:T(8,128)} %get-tuple-element.14.refs_2_, ...), custom_call_target="tpu_custom_call" | custom-call | tf_op jit(solution)/shard_map/pallas_call | solution.py:536

commit v5 on v4

--- a/solution.py
+++ b/solution.py
@@ -395,11 +395,6 @@
     grads_three()
     side_sent(1, 3)
     grads_two(0)
-    rows_two(0)
-    grads_four()
-    rows_two(1)
-    adam()
-
     wanted = lax.broadcasted_iota(I32, (64, 128), 0)
     table = jnp.zeros((64, 128), F32)
     loads["ids"].wait()
@@ -413,21 +408,33 @@
         table = table + jnp.where(wanted == code, 1.0, 0.0)
     table = table.astype(BF16)
 
-    for u in range(n_units):
+    def gather_fin(u):
         for rep in (0, 1):
             for ll in (yl, 1 - yl):
                 for cc in (c, sib):
                     if rep == 1 or ll is not yl or cc is not c:
                         arrived(fin[u].at[rep, cc, ll], s_fin + 8 * u + 4 * rep + 2 * cc + ll)
+
+    def natural_of(u, rep, cc):
+        total = jnp.zeros((64, CH), F32)
+        for par in (0, 1):
+            total += jnp.dot(
+                fin[u][rep, cc, :, par].reshape(64, WIDTHS[u]), place[par, pl.ds(PLACES[u], WIDTHS[u])],
+                preferred_element_type=F32,
+            )
+        return total
+
+    rows_two(0)
+    grads_four()
+    rows_two(1)
+    gather_fin(0)
+    early = [natural_of(0, rep, cc) for rep in (0, 1) for cc in (0, 1)]
+    adam()
+
+    gather_fin(1)
     for rep in (0, 1):
         for cc in (0, 1):
-            natural = jnp.zeros((64, CH), F32)
-            for u in range(n_units):
-                for par in (0, 1):
-                    natural += jnp.dot(
-                        fin[u][rep, cc, :, par].reshape(64, WIDTHS[u]), place[par, pl.ds(PLACES[u], WIDTHS[u])],
-                        preferred_element_type=F32,
-                    )
+            natural = early[2 * rep + cc] + natural_of(1, rep, cc)
             from_x = (x, xp)[rep]
             chunk = (from_x, 3 - from_x)[cc]
             out_ref[rep, cc] = lax.dot_general(

time: 57.2 us -> 56.7 us (level)
  no operation moved by 1% of the time
where the time goes in v5:
time: 56.7 us; the launch traced here: 56.5 us
  Pallas kernels  55.9 us (99%)
  between operations  0.64 us (1%)
    pallas_call x1, Pallas kernels, body(): pl.pallas_call(kernel, out_shape=(jax.ShapeDtypeStruct((128, D), BF16), s...  53.5 us
    pallas_call x1, Pallas kernels, body(): pl.pallas_call(hand_over, out_shape=(jax.ShapeDtypeStruct((128, D), BF16)...  2.39 us

profile of v5, /device:TPU:1, one launch (start us, length us, event | category | flops | bytes accessed | tf_op | source)
XLA Modules:
  0.0 56.5 jit_solution(14691084510456364271)
XLA Ops:
  0.6 53.5 %shard_map.111 = (bf16[128,3584]{1,0:T(8,128)(2,1)}, f32[224,256]{1,0:T(8,128)}, f32[224,256]{1,0:T(8,128)}, f32[224,256]{1,0:T(8,128)}) custom-call(bf16[320,3584]{1,0:T(8,128)(2,1)} %x_hbm.1, bf16[320,256]{1,0:T(8,128)(2,1)} %hg_hbm.1, s32[1,32]{1,0:T(1,128)} %bitcast.14, s32[8,128]{1,0:T(8,128)} %bitcast.12, s32[8,128]{1,0:T(8,128)} %bitcast.13, ...), custom_call_target="tpu_custom_call" | custom-call | tf_op jit(solution)/shard_map/pallas_call | solution.py:495
  54.2 2.4 %shard_map.112 = (bf16[128,3584]{1,0:T(8,128)(2,1)}, f32[224,256]{1,0:T(8,128)}, f32[224,256]{1,0:T(8,128)}, f32[224,256]{1,0:T(8,128)}) custom-call(bf16[128,3584]{1,0:T(8,128)(2,1)} %get-tuple-element.12.refs_0_, f32[224,256]{1,0:T(8,128)} %get-tuple-element.13.refs_1_, f32[224,256]{1,0:T(8,128)} %get-tuple-element.14.refs_2_, ...), custom_call_target="tpu_custom_call" | custom-call | tf_op jit(solution)/shard_map/pallas_call | solution.py:543
